TPU v7x, 32 devices: a whole 2x2x4 slice. The times are simulated.
32 devices in a mesh: ctx: 8 (over y, x, core), exp: 4 (over z).
Axes of the slice: x: 2, y: 2, z: 4, core: 2. Of those that a mesh axis runs over, the one named last changes fastest.
Arguments:
- residual: bfloat16 [1024, 4096], P(('ctx', 'exp')), may hold values from -6 to 6
- queries: bfloat16 [1024, 4096], P('ctx', 'exp'), may hold values from -8 to 8
- keys: bfloat16 [1024, 256], P('ctx'), may hold values from -8 to 8
- values: bfloat16 [1024, 256], P('ctx'), may hold values from -6 to 6
- span_pos: int32 [16], replicated, may hold values from 0 to 15, each once
- out_proj: bfloat16 [4096, 4096], P('exp'), may hold values from -0.71875 to 0.71875
- norm_gain: float32 [4096], replicated, may hold values from 0.25 to 1.75
- expert_gate: bfloat16 [16, 4096, 768], P('exp', None, 'ctx'), may hold values from -0.09375 to 0.09375
- expert_up: bfloat16 [16, 4096, 768], P('exp', None, 'ctx'), may hold values from -0.09375 to 0.09375
- expert_ids: int32 [1024, 8], P(('ctx', 'exp')), may hold values from 0 to 15, all different within a row; in each aligned block of 32 rows (0 to 31, 32 to 63, ...) at most 24 rows name the same one
- route_weight: float32 [1024, 8], P(('ctx', 'exp')), may hold values from 0.25 to 2
Outputs:
- mixed: bfloat16 [1024, 4096], P(('ctx', 'exp'))
- routed: bfloat16 [1024, 8, 768], P(('ctx', 'exp'))
Inputs may be any that keep to these rules, and one draw needn't show every extreme that they name: `span_pos`: every span number appears once. `expert_ids`: each row names 8 different experts; among the rows of one device (32 rows in a row, aligned) no expert is named more than 24 times, and in some device's rows some expert is named exactly 24 times.
All inputs are finite; a program needn't handle non-finite values.
Results may differ from a plain program's by a relative error of at most 0.035.
Values may be sent and summed in bfloat16 or wider, within the bound.
A program may use at most 192 MiB of HBM per device.

v0:
```python
import math

import jax
import jax.numpy as jnp
from jax import lax
from jax.sharding import PartitionSpec as P

D = 4096
HQ = 32
KVH = 2
HD = 128
FE = 768
EXPERTS = 16
TOPK = 8
CH = 64


def stored_positions(span_pos, first, count):
    rows = first + jnp.arange(count, dtype=jnp.int32)
    span = rows // CH
    table = span[:, None] == jnp.arange(span_pos.shape[0], dtype=jnp.int32)[None, :]
    base = jnp.sum(jnp.where(table, span_pos[None, :], 0), axis=1)
    return base * CH + rows % CH


def hidden_units(rows_in, weight_pair):
    gate = jnp.einsum(
        "esd,edf->esf", rows_in, weight_pair[:, 0], preferred_element_type=jnp.float32
    )
    upper = jnp.einsum(
        "esd,edf->esf", rows_in, weight_pair[:, 1], preferred_element_type=jnp.float32
    )
    return jax.nn.silu(gate) * upper


def shards(
    residual,
    queries,
    keys,
    values,
    span_pos,
    out_proj,
    norm_gain,
    expert_gate,
    expert_up,
    expert_ids,
    route_weight,
):
    weight_pair = jnp.stack((expert_gate, expert_up), axis=1)
    tok_rows = queries.shape[0]
    per_device = queries.shape[1] // HD
    group = HQ // KVH
    ctx_index = lax.axis_index("ctx")
    exp_index = lax.axis_index("exp")
    kv_head = exp_index * per_device // group
    own_keys = lax.dynamic_slice_in_dim(keys, kv_head * HD, HD, 1)
    own_values = lax.dynamic_slice_in_dim(values, kv_head * HD, HD, 1)
    query_pos = stored_positions(span_pos, ctx_index * tok_rows, tok_rows)
    query_heads = queries.reshape(tok_rows, per_device, HD)
    scale = 1.0 / math.sqrt(HD)
    start_carry = (
        jnp.full((per_device, tok_rows), -1e30, jnp.float32),
        jnp.zeros((per_device, tok_rows), jnp.float32),
        jnp.zeros((per_device, tok_rows, HD), jnp.float32),
    )
    carry = start_carry
    start = jnp.int32(0)
    key_piece = lax.all_gather(own_keys, "ctx", axis=0, tiled=True)
    value_piece = lax.all_gather(own_values, "ctx", axis=0, tiled=True)
    length = key_piece.shape[0]
    block = min(length, 1024)
    for begin in range(0, length, block):
        stop = min(begin + block, length)
        attend_key_piece = key_piece[begin:stop]
        attend_value_piece = value_piece[begin:stop]
        attend_start = start + begin
        attend_running, attend_total, attend_accum = carry
        key_pos = stored_positions(span_pos, attend_start, attend_key_piece.shape[0])
        scores = (
            jnp.einsum(
                "tqd,nd->qtn", query_heads, attend_key_piece, preferred_element_type=jnp.float32
            )
            * scale
        )
        visible = key_pos[None, None, :] <= query_pos[None, :, None]
        block_top = jnp.max(jnp.where(visible, scores, -1e30), axis=2)
        new_top = jnp.maximum(attend_running, block_top)
        factor = jnp.exp(attend_running - new_top)
        probs = jnp.where(visible, jnp.exp(scores - new_top[:, :, None]), 0.0)
        attend_total = attend_total * factor + jnp.sum(probs, axis=2)
        summed = jnp.einsum(
            "qtn,nd->qtd",
            probs.astype(jnp.bfloat16),
            attend_value_piece,
            preferred_element_type=jnp.float32,
        )
        attend_accum = attend_accum * factor[:, :, None] + summed
        carry = (new_top, attend_total, attend_accum)
    running, total, accum = carry
    attn = (accum / total[:, :, None]).astype(jnp.bfloat16)
    attn = jnp.transpose(attn, (1, 0, 2)).reshape(tok_rows, per_device * HD)
    tok_dev = residual.shape[0]
    head_total = lax.psum_scatter(
        jnp.dot(attn, out_proj, preferred_element_type=jnp.float32).astype(jnp.bfloat16),
        "exp",
        scatter_dimension=0,
        tiled=True,
    ).astype(jnp.float32)
    mixed = (residual.astype(jnp.float32) + head_total).astype(jnp.bfloat16)
    mixed_f = mixed.astype(jnp.float32)
    square = jnp.mean(mixed_f * mixed_f, axis=1, keepdims=True)
    normed = (mixed_f * lax.rsqrt(square + 1e-06) * norm_gain[None, :]).astype(jnp.bfloat16)
    most_slots = 3 * tok_dev // 4
    ids_flat = expert_ids.reshape(-1)
    onehot = (ids_flat[:, None] == jnp.arange(EXPERTS, dtype=jnp.int32)[None, :]).astype(jnp.int32)
    earlier = jnp.cumsum(onehot, axis=0) - onehot
    slot = jnp.sum(earlier * onehot, axis=1)
    target = ids_flat * most_slots + slot
    placing = (
        target[:, None] == jnp.arange(EXPERTS * most_slots, dtype=jnp.int32)[None, :]
    ).astype(jnp.bfloat16)
    placing = jnp.sum(placing.reshape(tok_dev, TOPK, EXPERTS * most_slots), axis=1)
    outgoing = jnp.einsum("ts,td->sd", placing, normed, preferred_element_type=jnp.float32).astype(
        jnp.bfloat16
    )
    outgoing = outgoing.reshape(EXPERTS, most_slots, D)
    received = lax.all_to_all(outgoing, "exp", split_axis=0, concat_axis=1, tiled=True)
    hidden = hidden_units(received, lax.all_gather(weight_pair, "ctx", axis=3, tiled=True))
    returned = (
        lax.all_to_all(hidden.astype(jnp.bfloat16), "exp", split_axis=1, concat_axis=0, tiled=True)
        .astype(hidden.dtype)
        .reshape(EXPERTS * most_slots, FE)
    )
    picked = jnp.take(returned, target, axis=0)
    routed = (picked * route_weight.reshape(-1)[:, None]).astype(jnp.bfloat16)
    return (mixed, routed.reshape(tok_dev, TOPK, FE))


def solution(mesh):
    in_specs = (
        P(("ctx", "exp"), None),
        P("ctx", "exp"),
        P("ctx", None),
        P("ctx", None),
        P(),
        P("exp", None),
        P(),
        P("exp", None, "ctx"),
        P("exp", None, "ctx"),
        P(("ctx", "exp"), None),
        P(("ctx", "exp"), None),
    )
    out_specs = (P(("ctx", "exp"), None), P(("ctx", "exp"), None, None))
    return jax.shard_map(shards, mesh=mesh, in_specs=in_specs, out_specs=out_specs, check_vma=False)
```

profile of v0, /device:TPU:0, one launch (start us, length us, event | category | flops | bytes accessed | tf_op | source)
XLA Modules:
  0.0 463.0 jit_solution(14844206075028913362)
XLA Ops:
  8.0 0.0 copy-start
  8.0 0.0 reduce-scatter.2.cloned.1.call-start
  8.1 0.8 constant_dynamic-slice_fusion.1
  8.9 10.8 %all_gather.9 = bf16[1024,128]{1,0:T(8,128)(2,1)S(1)} all-gather(bf16[128,128]{1,0:T(8,128)(2,1)S(1)} %constant_dynamic-slice_fusion.1), channel_id=1, replica_groups=mesh['ctx'=8,'exp'=4] {'ctx'}, dimensions={0}, use_global_device_ids=true | all-gather | bytes 294912 | tf_op jit(solution)/shard_map/all_gather | solution.py:68
  19.6 0.7 select_reduce_fusion.1
  20.4 0.7 select_reduce_fusion
  21.1 0.2 broadcast_compare_fusion
  21.4 0.0 copy-start.6
  21.4 0.8 fusion.4
  22.2 1.9 copy-done.2
  24.1 0.9 fusion.7
  25.0 0.1 copy.66
  25.1 9.4 %all_gather.10 = bf16[1024,128]{0,1:T(8,128)(2,1)S(1)} all-gather(bf16[128,128]{0,1:T(8,128)(2,1)S(1)} %copy.66), channel_id=1, replica_groups=mesh['ctx'=8,'exp'=4] {'ctx'}, dimensions={0}, use_global_device_ids=true | all-gather | bytes 294912 | tf_op jit(solution)/shard_map/all_gather | solution.py:69
  34.4 3.1 fusion.27
  37.6 5.7 %convolution_convert_fusion.1 = bf16[128,4096]{1,0:T(8,128)(2,1)} fusion(bf16[128,1024]{0,1:T(8,128)(2,1)S(1)} %bitcast.116, bf16[1024,4096]{1,0:T(8,128)(2,1)} %param.16), kind=kOutput, calls=%fused_computation.7 | convolution fusion | flops 1074266112 | bytes 9699328 | tf_op jit(solution)/shard_map/dot_general | solution.py:104
  43.2 0.0 reduce-scatter.2.cloned.1.call-update
  43.3 0.2 all-gather.2.cloned.1.call-start
  43.5 8.1 %copy_bitcast_fusion = (bf16[4,1,4096,96]{2,0,1,3:T(4,128)(2,1)S(1)}, bf16[4,1,4096,96]{2,0,1,3:T(4,128)(2,1)S(1)}) fusion(bf16[4,4096,96]{1,2,0:T(8,128)(2,1)} %param.19, bf16[4,4096,96]{1,2,0:T(8,128)(2,1)} %param.18), kind=kLoop, calls=%fused_computation.15 | loop fusion | bytes 12582912 | tf_op jit(solution)/shard_map/stack | solution.py:49
  51.6 6.6 %pad_maximum_fusion = bf16[4,2,4096,96]{2,0,1,3:T(4,128)(2,1)} fusion(bf16[4,1,4096,96]{2,0,1,3:T(4,128)(2,1)S(1)} %get-tuple-element.12, bf16[4,1,4096,96]{2,0,1,3:T(4,128)(2,1)S(1)} %get-tuple-element.13), kind=kLoop, calls=%fused_computation.5 | loop fusion | flops 3145728 | bytes 12582912 | tf_op jit(solution)/shard_map/stack | solution.py:49
  58.3 0.0 all-gather.2.cloned.1.call-update
  58.3 0.7 copy-done.7
  58.9 0.1 copy.53
  59.0 0.1 eq.76
  59.1 0.1 reshape.222
  59.2 0.6 reduce-window.6
  59.8 0.2 slice_reduce_fusion
  60.0 0.1 fusion.47
  60.1 0.1 reduce_sum.68
  60.2 0.2 fusion.44
  60.4 10.4 %reduce-scatter.2.cloned.1.call-done = bf16[32,4096]{1,0:T(8,128)(2,1)} async-done(((bf16[128,4096]{1,0:T(8,128)(2,1)}), bf16[32,4096]{1,0:T(8,128)(2,1)}) %reduce-scatter.2.cloned.1.call-update) | async-done | bytes 262160 | tf_op jit(solution)/shard_map/reduce_scatter | solution.py:103
  70.9 1.2 fusion.32
  72.1 1.0 convolution_convert_fusion
  73.2 73.3 %all_to_all.27 = bf16[16,24,4096]{2,1,0:T(8,128)(2,1)S(1)} all-to-all(bf16[16,24,4096]{2,1,0:T(8,128)(2,1)S(1)} %bitcast.113), channel_id=1, replica_groups=mesh['ctx'=8,'exp'=4] {'exp'}, dimensions={0} | all-to-all | bytes 6291456 | tf_op jit(solution)/shard_map/all_to_all | solution.py:127
  146.4 0.2 copy.57
  146.6 144.1 %all-gather.2.cloned.1.call-done = bf16[4,2,4096,768]{2,0,1,3:T(4,128)(2,1)} async-done(((bf16[4,2,4096,96]{2,0,1,3:T(4,128)(2,1)}), bf16[4,2,4096,768]{2,0,1,3:T(4,128)(2,1)}) %all-gather.2.cloned.1.call-update) | async-done | bytes 50331664 | tf_op jit(solution)/shard_map/all_gather | solution.py:128
  290.7 40.8 %fusion.62 = (bf16[4,1,4096,768]{2,0,1,3:T(4,128)(2,1)}, bf16[4,1,4096,768]{2,0,1,3:T(4,128)(2,1)}) fusion(bf16[4,2,4096,768]{2,0,1,3:T(4,128)(2,1)} %all-gather.2.cloned.1.call-done), kind=kLoop, calls=%fused_computation.91 | loop fusion | bytes 100663296 | tf_op jit(solution)/shard_map/slice | solution.py:28
  331.5 38.8 %copy.67 = bf16[4,1,4096,768]{3,2,0,1:T(8,128)(2,1)} copy(bf16[4,1,4096,768]{2,0,1,3:T(4,128)(2,1)} %get-tuple-element.6) | data formatting | bytes 50331648
  370.3 38.7 %copy.68 = bf16[4,1,4096,768]{3,2,0,1:T(8,128)(2,1)} copy(bf16[4,1,4096,768]{2,0,1,3:T(4,128)(2,1)} %get-tuple-element.7) | data formatting | bytes 50331648
  409.0 10.2 %fusion.2 = f32[4,96,768]{2,1,0:T(8,128)S(1)} fusion(bf16[4,96,4096]{2,1,0:T(8,128)(2,1)S(1)} %bitcast.110, bf16[4,1,4096,768]{3,2,0,1:T(8,128)(2,1)} %copy.67), kind=kOutput, calls=%fused_computation.3 | convolution fusion | flops 2415919104 | bytes 29491200 | tf_op jit(solution)/shard_map/esd,edf->esf/dot_general | solution.py:27
  419.2 12.1 %fusion.15 = bf16[4,96,768]{2,1,0:T(8,128)(2,1)S(1)} fusion(bf16[4,96,4096]{2,1,0:T(8,128)(2,1)S(1)} %bitcast.111, bf16[4,1,4096,768]{3,2,0,1:T(8,128)(2,1)} %copy.68, f32[4,96,768]{2,1,0:T(8,128)S(1)} %fusion.2), kind=kOutput, calls=%fused_computation.20 | convolution fusion | flops 2417688576 | bytes 30081024 | tf_op jit(solution)/shard_map/esd,edf->esf/dot_general | solution.py:30
  431.3 1.3 copy.62
  432.6 4.6 all-to-all-start.1
  437.2 0.1 mul.119
  437.3 0.1 copy.64
  437.4 16.1 %all-to-all-done.1 = bf16[4,96,768]{2,0,1:T(4,128)(2,1)S(1)} async-done(((bf16[4,96,768]{2,0,1:T(4,128)(2,1)}), bf16[4,96,768]{2,0,1:T(4,128)(2,1)S(1)}, u32[]{:S(2)}, u32[]{:S(2)}) %all-to-all-start.1) | async-done | bytes 589856 | tf_op jit(solution)/shard_map/all_to_all | solution.py:130
  453.5 0.1 copy.63
  453.6 1.1 gather_fusion
  454.7 0.9 fusion.31
  (29 shorter events, 0.2 us)
Async XLA Ops:
  8.0 13.4 %copy-start = (bf16[128,1024]{1,0:T(8,128)(2,1)S(1)}, bf16[128,1024]{1,0:T(8,128)(2,1)}, u32[]{:S(2)}) copy-start(bf16[128,1024]{1,0:T(8,128)(2,1)} %param.12) | copy-start | bytes 786436
  8.0 62.9 %reduce-scatter.2.cloned.1.call-start = ((), (), s32[]{:S(2)}) async-start(), calls=%async_computation.3 | async-start | bytes 1310720 | tf_op jit(solution)/shard_map/reduce_scatter | solution.py:103
  21.4 3.6 copy-start.6
  22.1 1.9 copy-start.2
  43.3 247.5 %all-gather.2.cloned.1.call-start = ((), (), s32[]{:S(2)}) async-start(), calls=%async_computation.4 | async-start | bytes 56623104 | tf_op jit(solution)/shard_map/all_gather | solution.py:128
  58.3 0.7 copy-start.7
  58.3 12.6 %copy-start.4 = (bf16[32,4096]{1,0:T(8,128)(2,1)S(1)}, bf16[32,4096]{1,0:T(8,128)(2,1)}, u32[]{:S(2)}) copy-start(bf16[32,4096]{1,0:T(8,128)(2,1)} %param.11) | copy-start | bytes 786436
  58.3 13.9 %copy-start.5 = (f32[4096]{0:T(1024)S(1)}, f32[4096]{0:T(1024)}, u32[]{:S(2)}) copy-start(f32[4096]{0:T(1024)} %param.17) | copy-start | bytes 49156
  72.1 74.3 %copy-start.3 = (bf16[32,4096]{1,0:T(8,128)(2,1)}, bf16[32,4096]{1,0:T(8,128)(2,1)S(1)}, u32[]{:S(2)}) copy-start(bf16[32,4096]{1,0:T(8,128)(2,1)S(1)} %get-tuple-element.5) | copy-start | bytes 786436
  419.2 18.1 %copy-start.8 = (f32[32,8]{0,1:T(8,128)S(1)}, f32[32,8]{0,1:T(8,128)}, u32[]{:S(2)}) copy-start(f32[32,8]{0,1:T(8,128)} %param.21) | copy-start | bytes 3076
  432.6 20.9 %all-to-all-start.1 = ((bf16[4,96,768]{2,0,1:T(4,128)(2,1)}), bf16[4,96,768]{2,0,1:T(4,128)(2,1)S(1)}, u32[]{:S(2)}, u32[]{:S(2)}) async-start(bf16[4,96,768]{2,0,1:T(4,128)(2,1)} %copy.62), calls=%async_computation.2 | async-start | bytes 1179648 | tf_op jit(solution)/shard_map/all_to_all | solution.py:130
  453.5 2.1 copy-start.1
Sparse Core Ops, SparseCore 0:
  43.4 27.4 reduce-scatter.1
Sparse Core Ops, SparseCore 1:
  58.4 232.3 all-gather.1
where the time goes:
time: 465 us; the launch traced here: 463 us
  waiting for transfers between devices  171 us (37%)
  local copies, waits for them, and re-layouts  133 us (29%)
  blocking collectives  93.4 us (20%)
  matrix products  32.9 us (7%)
  between operations  15.7 us (3%)
  other arithmetic  12.3 us (3%)
  starting transfers between devices  4.85 us (1%)
    all_gather x1, waiting for transfers between devices, shards(): lax.all_gather(weight_pair, 'ctx', axis=3, tiled=True)  144 us
    unnamed x23, local copies, waits for them, and re-layouts  80.4 us
    all_to_all x1, blocking collectives, shards(): lax.all_to_all(outgoing, 'exp', split_axis=0, concat_axis=1, tiled=True)  73.3 us
    slice x1, local copies, waits for them, and re-layouts, hidden_units(): weight_pair[:, 0]  40.8 us
    all_to_all x1, waiting for transfers between devices, shards(): lax.all_to_all(hidden.astype(jnp.bfloat16), 'exp', split_axis=1, concat_a...  16.1 us
    dot_general x1, matrix products, hidden_units(): jnp.einsum('esd,edf->esf', rows_in, weight_pair[:, 1], preferred_element_...  12.1 us
    all_gather x1, blocking collectives, shards(): key_piece = lax.all_gather(own_keys, 'ctx', axis=0, tiled=True)  10.8 us
    reduce_scatter x1, waiting for transfers between devices, shards(): lax.psum_scatter(jnp.dot(attn, out_proj, preferred_element_type=jnp.float...  10.4 us
  transfers between devices with their start and end apart: 3, of which 3 were waited for; matrix products, arithmetic and copies ran while one was open for 4% of the time, Pallas kernels for 0%

commit v1 on v0

--- a/solution.py
+++ b/solution.py
@@ -23,16 +23,6 @@
     return base * CH + rows % CH
 
 
-def hidden_units(rows_in, weight_pair):
-    gate = jnp.einsum(
-        "esd,edf->esf", rows_in, weight_pair[:, 0], preferred_element_type=jnp.float32
-    )
-    upper = jnp.einsum(
-        "esd,edf->esf", rows_in, weight_pair[:, 1], preferred_element_type=jnp.float32
-    )
-    return jax.nn.silu(gate) * upper
-
-
 def shards(
     residual,
     queries,
@@ -46,7 +36,6 @@
     expert_ids,
     route_weight,
 ):
-    weight_pair = jnp.stack((expert_gate, expert_up), axis=1)
     tok_rows = queries.shape[0]
     per_device = queries.shape[1] // HD
     group = HQ // KVH
@@ -65,8 +54,10 @@
     )
     carry = start_carry
     start = jnp.int32(0)
-    key_piece = lax.all_gather(own_keys, "ctx", axis=0, tiled=True)
-    value_piece = lax.all_gather(own_values, "ctx", axis=0, tiled=True)
+    key_value = lax.all_gather(
+        jnp.concatenate((own_keys, own_values), axis=1), "ctx", axis=0, tiled=True
+    )
+    key_piece, value_piece = key_value[:, :HD], key_value[:, HD:]
     length = key_piece.shape[0]
     block = min(length, 1024)
     for begin in range(0, length, block):
@@ -110,28 +101,27 @@
     mixed_f = mixed.astype(jnp.float32)
     square = jnp.mean(mixed_f * mixed_f, axis=1, keepdims=True)
     normed = (mixed_f * lax.rsqrt(square + 1e-06) * norm_gain[None, :]).astype(jnp.bfloat16)
-    most_slots = 3 * tok_dev // 4
-    ids_flat = expert_ids.reshape(-1)
-    onehot = (ids_flat[:, None] == jnp.arange(EXPERTS, dtype=jnp.int32)[None, :]).astype(jnp.int32)
-    earlier = jnp.cumsum(onehot, axis=0) - onehot
-    slot = jnp.sum(earlier * onehot, axis=1)
-    target = ids_flat * most_slots + slot
-    placing = (
-        target[:, None] == jnp.arange(EXPERTS * most_slots, dtype=jnp.int32)[None, :]
-    ).astype(jnp.bfloat16)
-    placing = jnp.sum(placing.reshape(tok_dev, TOPK, EXPERTS * most_slots), axis=1)
-    outgoing = jnp.einsum("ts,td->sd", placing, normed, preferred_element_type=jnp.float32).astype(
-        jnp.bfloat16
+    every = lax.all_gather(normed, ("ctx", "exp"), axis=0, tiled=True)
+    experts, _, width = expert_gate.shape
+    devices = every.shape[0] // tok_dev
+    weights = jnp.transpose(jnp.stack((expert_gate, expert_up)), (2, 0, 1, 3))
+    units = jnp.dot(
+        every, weights.reshape(D, 2 * experts * width), preferred_element_type=jnp.float32
     )
-    outgoing = outgoing.reshape(EXPERTS, most_slots, D)
-    received = lax.all_to_all(outgoing, "exp", split_axis=0, concat_axis=1, tiled=True)
-    hidden = hidden_units(received, lax.all_gather(weight_pair, "ctx", axis=3, tiled=True))
-    returned = (
-        lax.all_to_all(hidden.astype(jnp.bfloat16), "exp", split_axis=1, concat_axis=0, tiled=True)
-        .astype(hidden.dtype)
-        .reshape(EXPERTS * most_slots, FE)
+    gate, upper = units[:, : experts * width], units[:, experts * width :]
+    hidden = (jax.nn.silu(gate) * upper).astype(jnp.bfloat16)
+    returned = lax.all_to_all(
+        hidden.reshape(devices, tok_dev, experts * width),
+        ("ctx", "exp"),
+        split_axis=0,
+        concat_axis=0,
+        tiled=True,
     )
-    picked = jnp.take(returned, target, axis=0)
+    n_exp = EXPERTS // experts
+    returned = returned.reshape(devices // n_exp, n_exp, tok_dev, experts, width)
+    returned = jnp.transpose(returned, (2, 1, 3, 0, 4)).reshape(tok_dev * EXPERTS, FE)
+    target = jnp.arange(tok_dev, dtype=jnp.int32)[:, None] * EXPERTS + expert_ids
+    picked = jnp.take(returned, target.reshape(-1), axis=0).astype(jnp.float32)
     routed = (picked * route_weight.reshape(-1)[:, None]).astype(jnp.bfloat16)
     return (mixed, routed.reshape(tok_dev, TOPK, FE))
 

time: 465 us -> 183 us (0.39)
  local copies, waits for them, and re-layouts: 133 us -> 6.78 us
  blocking collectives: 93.4 us -> 11.3 us
  waiting for transfers between devices: 171 us -> 119 us
  matrix products: 32.9 us -> 14.9 us
    unnamed x23 -> x17, local copies, waits for them, and re-layouts: 80.4 us -> 1.84 us
    all_to_all x1 -> x0, blocking collectives: 73.3 us -> none  [shards(): lax.all_to_all(outgoing, 'exp', split_axis=0, concat_axis=1, tiled=True)]
    all_gather x1, waiting for transfers between devices: 144 us -> 72 us  [shards(): every = lax.all_gather(normed, ('ctx', 'exp'), axis=0, tiled=True)]
    slice x2 -> x0, local copies, waits for them, and re-layouts: 40.9 us -> none  [the longest x1 40.8 us: hidden_units(): weight_pair[:, 0]]
    reduce_scatter x1, waiting for transfers between devices: 10.4 us -> 27.6 us  [shards(): lax.psum_scatter(jnp.dot(attn, out_proj, preferred_element_type=jnp.float...]
    dot_general x3 -> x1, matrix products: 23.3 us -> 11 us  [shards(): jnp.dot(every, weights.reshape(D, 2 * experts * width), preferred_element...]
    all_gather x2 -> x1, blocking collectives: 20.1 us -> 11.3 us  [shards(): lax.all_gather(jnp.concatenate((own_keys, own_values), axis=1), 'ctx', ax...]
    another operation x2 -> x0, local copies, waits for them, and re-layouts: 8.12 us -> none  [the longest x1 8.11 us: shards(): weight_pair = jnp.stack((expert_gate, expert_up), axis=1)]
  transfers between devices with their start and end apart: 3 -> 3, of which waited for: 3 -> 3; matrix products, arithmetic and copies ran while one was open for 4% -> 3% of each run, Pallas kernels for 0% -> 0%
where the time goes in v1:
time: 183 us; the launch traced here: 182 us
  waiting for transfers between devices  119 us (65%)
  matrix products  14.9 us (8%)
  between operations  14.3 us (8%)
  other arithmetic  12.1 us (7%)
  blocking collectives  11.3 us (6%)
  local copies, waits for them, and re-layouts  6.78 us (4%)
  starting transfers between devices  3.45 us (2%)
    all_gather x1, waiting for transfers between devices, shards(): every = lax.all_gather(normed, ('ctx', 'exp'), axis=0, tiled=True)  72 us
    reduce_scatter x1, waiting for transfers between devices, shards(): lax.psum_scatter(jnp.dot(attn, out_proj, preferred_element_type=jnp.float...  27.6 us
    all_to_all x1, waiting for transfers between devices, shards(): lax.all_to_all(hidden.reshape(devices, tok_dev, experts * width), ('ctx',...  19 us
    all_gather x1, blocking collectives, shards(): lax.all_gather(jnp.concatenate((own_keys, own_values), axis=1), 'ctx', ax...  11.3 us
    dot_general x1, matrix products, shards(): jnp.dot(every, weights.reshape(D, 2 * experts * width), preferred_element...  11 us
    another operation x1, other arithmetic, shards(): weights = jnp.transpose(jnp.stack((expert_gate, expert_up)), (2, 0, 1, 3))  5.17 us
  transfers between devices with their start and end apart: 3, of which 3 were waited for; matrix products, arithmetic and copies ran while one was open for 3% of the time, Pallas kernels for 0%

profile of v1, /device:TPU:0, one launch (start us, length us, event | category | flops | bytes accessed | tf_op | source)
XLA Modules:
  0.0 181.6 jit_solution(17414026698298705223)
XLA Ops:
  7.2 0.0 copy-start
  7.2 0.0 reduce-scatter.2.cloned.1.call-start
  7.3 0.8 constant_dynamic-slice_fusion
  8.1 11.3 %all_gather.6 = bf16[1024,256]{1,0:T(8,128)(2,1)S(1)} all-gather(bf16[128,256]{1,0:T(8,128)(2,1)S(1)} %pad_maximum_fusion.1), channel_id=1, replica_groups=mesh['ctx'=8,'exp'=4] {'ctx'}, dimensions={0}, use_global_device_ids=true | all-gather | bytes 589824 | tf_op jit(solution)/shard_map/all_gather | solution.py:57
  19.4 0.7 select_reduce_fusion.1
  20.1 0.7 select_reduce_fusion
  20.9 0.2 broadcast_compare_fusion
  21.1 0.0 copy-done
  21.1 0.0 slice-start
  21.1 0.8 fusion
  21.9 0.0 slice-start.1
  21.9 0.9 fusion.3
  22.8 0.9 fusion.18
  23.7 0.0 slice-done
  23.8 1.0 slice-done.1
  24.8 0.0 copy-start.3
  24.8 0.0 copy-start.1
  24.8 2.3 %convolution_convert_fusion = bf16[128,4096]{1,0:T(8,128)(2,1)} fusion(bf16[128,1024]{0,1:T(8,128)(2,1)S(1)} %bitcast.80, bf16[1024,4096]{1,0:T(8,128)(2,1)S(1)} %bitcast.75), kind=kOutput, calls=%fused_computation.2 | convolution fusion | flops 1074266112 | bytes 9699328 | tf_op jit(solution)/shard_map/dot_general | solution.py:95
  27.1 0.0 reduce-scatter.2.cloned.1.call-update
  27.1 0.0 all-gather.2.cloned.1.call-start
  27.1 27.6 %reduce-scatter.2.cloned.1.call-done = bf16[32,4096]{1,0:T(8,128)(2,1)} async-done(((bf16[128,4096]{1,0:T(8,128)(2,1)}), bf16[32,4096]{1,0:T(8,128)(2,1)}) %reduce-scatter.2.cloned.1.call-update) | async-done | bytes 262160 | tf_op jit(solution)/shard_map/reduce_scatter | solution.py:94
  54.7 1.2 fusion.21
  55.9 0.0 copy-start.2
  56.0 0.7 copy-done.2
  56.6 0.0 copy-done.3
  56.7 0.8 fusion.23
  57.5 0.0 all-gather.2.cloned.1.call-update
  57.5 0.0 copy-done.1
  57.5 5.2 %pad_maximum_fusion = bf16[2,4,4096,96]{2,3,1,0:T(8,128)(2,1)} fusion(bf16[1,4,4096,96]{2,3,1,0:T(8,128)(2,1)S(1)} %bitcast.78, bf16[1,4,4096,96]{2,3,1,0:T(8,128)(2,1)} %bitcast.79), kind=kLoop, calls=%fused_computation.1 | loop fusion | flops 3145728 | bytes 12582912 | tf_op jit(solution)/shard_map/stack | solution.py:107
  62.7 72.0 %all-gather.2.cloned.1.call-done = bf16[1024,4096]{1,0:T(8,128)(2,1)} async-done(((bf16[32,4096]{1,0:T(8,128)(2,1)}), bf16[1024,4096]{1,0:T(8,128)(2,1)}) %all-gather.2.cloned.1.call-update) | async-done | bytes 8388624 | tf_op jit(solution)/shard_map/all_gather | solution.py:104
  134.7 11.0 %fusion.38 = f32[1024,768]{1,0:T(8,128)S(1)} fusion(bf16[1024,4096]{1,0:T(8,128)(2,1)} %all-gather.2.cloned.1.call-done, bf16[4096,768]{0,1:T(8,128)(2,1)} %bitcast.76), kind=kOutput, calls=%fused_computation.71 | convolution fusion | flops 6442450944 | bytes 17825792 | tf_op jit(solution)/shard_map/dot_general | solution.py:108
  145.7 0.0 copy-start.5
  145.7 0.0 copy-start.4
  145.7 1.3 fusion.8
  147.1 3.4 %all-to-all-start = ((bf16[32,32,384]{2,1,0:T(8,128)(2,1)}), bf16[32,32,384]{2,1,0:T(8,128)(2,1)S(1)}, u32[]{:S(2)}, u32[]{:S(2)}) async-start(bf16[32,32,384]{2,1,0:T(8,128)(2,1)} %bitcast.11), calls=%async_computation.1 | async-start | bytes 1572864 | tf_op jit(solution)/shard_map/all_to_all | solution.py:113
  150.4 0.0 copy-done.5
  150.5 0.1 copy.31
  150.5 0.1 reshape.201
  150.6 0.1 copy.29
  150.7 0.0 copy-done.4
  150.7 0.1 copy.32
  150.8 19.0 %all-to-all-done = bf16[32,32,384]{2,1,0:T(8,128)(2,1)S(1)} async-done(((bf16[32,32,384]{2,1,0:T(8,128)(2,1)}), bf16[32,32,384]{2,1,0:T(8,128)(2,1)S(1)}, u32[]{:S(2)}, u32[]{:S(2)}) %all-to-all-start) | async-done | bytes 786464 | tf_op jit(solution)/shard_map/all_to_all | solution.py:113
  169.9 0.6 reshape.199
  170.5 1.2 copy.44
  171.7 0.9 reshape.200
  172.6 1.2 gather_fusion
  173.8 0.9 multiply_convert_fusion
  (13 shorter events, 0.1 us)
Async XLA Ops:
  7.2 13.9 %copy-start = (bf16[128,1024]{1,0:T(8,128)(2,1)S(1)}, bf16[128,1024]{1,0:T(8,128)(2,1)}, u32[]{:S(2)}) copy-start(bf16[128,1024]{1,0:T(8,128)(2,1)} %param.12) | copy-start | bytes 786436
  7.2 47.5 %reduce-scatter.2.cloned.1.call-start = ((), (), s32[]{:S(2)}) async-start(), calls=%async_computation.2 | async-start | bytes 1310720 | tf_op jit(solution)/shard_map/reduce_scatter | solution.py:94
  21.1 2.6 %slice-start = ((s8[8388608]{0:T(1024)(128)(4,1)}), s8[4194304]{0:T(1024)(128)(4,1)S(1)}, s32[]{:S(2)}) async-start(s8[8388608]{0:T(1024)(128)(4,1)} %bitcast.74), calls=%async_computation.4 | async-start | bytes 8388608
  21.9 2.9 %slice-start.1 = ((s8[8388608]{0:T(1024)(128)(4,1)}), s8[4194304]{0:T(1024)(128)(4,1)S(1)}, s32[]{:S(2)}) async-start(s8[8388608]{0:T(1024)(128)(4,1)} %bitcast.74), calls=%async_computation.5 | async-start | bytes 8388608
  24.8 31.9 %copy-start.3 = (f32[4096]{0:T(1024)S(1)}, f32[4096]{0:T(1024)}, u32[]{:S(2)}) copy-start(f32[4096]{0:T(1024)} %param.17) | copy-start | bytes 49156
  24.8 32.7 %copy-start.1 = (bf16[4,4096,96]{1,2,0:T(8,128)(2,1)S(1)}, bf16[4,4096,96]{1,2,0:T(8,128)(2,1)}, u32[]{:S(2)}) copy-start(bf16[4,4096,96]{1,2,0:T(8,128)(2,1)} %param.19) | copy-start | bytes 9437188
  27.1 107.6 %all-gather.2.cloned.1.call-start = ((), (), s32[]{:S(2)}) async-start(), calls=%async_computation.3 | async-start | bytes 8650752 | tf_op jit(solution)/shard_map/all_gather | solution.py:104
  55.9 0.7 copy-start.2
  145.7 4.7 %copy-start.5 = (s32[32,8]{0,1:T(8,128)S(1)}, s32[32,8]{0,1:T(8,128)}, u32[]{:S(2)}) copy-start(s32[32,8]{0,1:T(8,128)} %param.20) | copy-start | bytes 3076
  145.7 5.0 %copy-start.4 = (f32[32,8]{0,1:T(8,128)S(1)}, f32[32,8]{0,1:T(8,128)}, u32[]{:S(2)}) copy-start(f32[32,8]{0,1:T(8,128)} %param.21) | copy-start | bytes 3076
  147.1 22.8 %all-to-all-start = ((bf16[32,32,384]{2,1,0:T(8,128)(2,1)}), bf16[32,32,384]{2,1,0:T(8,128)(2,1)S(1)}, u32[]{:S(2)}, u32[]{:S(2)}) async-start(bf16[32,32,384]{2,1,0:T(8,128)(2,1)} %bitcast.11), calls=%async_computation.1 | async-start | bytes 1572864 | tf_op jit(solution)/shard_map/all_to_all | solution.py:113
Sparse Core Ops, SparseCore 0:
  27.2 27.4 reduce-scatter.1
  58.6 76.0 all-gather.1

commit v2 on v1

--- a/solution.py
+++ b/solution.py
@@ -1,8 +1,11 @@
+import functools
 import math
 
 import jax
 import jax.numpy as jnp
 from jax import lax
+from jax.experimental import pallas as pl
+from jax.experimental.pallas import tpu as pltpu
 from jax.sharding import PartitionSpec as P
 
 D = 4096
@@ -23,7 +26,307 @@
     return base * CH + rows % CH
 
 
+MESH = pl.DeviceIdType.MESH
+
+
+def ring_place(index):
+    upper, lower = index // 2, index % 2
+    return upper * 2 + (lower + upper) % 2
+
+
+def expert_kernel(
+    n_pos,
+    n_exp,
+    part,
+    residual,
+    gain,
+    own_weights,
+    mixed,
+    ret,
+    tokens,
+    units,
+    hidden,
+    sums,
+    weights,
+    w_sem,
+    sum_send,
+    sum_recv,
+    line_send,
+    line_recv,
+    ring_send,
+    ring_recv,
+    back_send,
+    back_recv,
+):
+    ctx, exp = lax.axis_index("ctx"), lax.axis_index("exp")
+    pos, parity = ctx // 2, ctx % 2
+    ring = ring_place(pos)
+    half = n_pos // 2
+    slots = n_pos * n_exp
+    mine = pos * n_exp + exp
+    tok_dev = residual.shape[0]
+    width = hidden.shape[3]
+
+    def device(place, index):
+        return (2 * place + parity, index)
+
+    def remote(src, dst, send, recv, target):
+        return pltpu.make_async_remote_copy(
+            src_ref=src,
+            dst_ref=dst,
+            send_sem=send,
+            recv_sem=recv,
+            device_id=target,
+            device_id_type=MESH,
+        )
+
+    partner = (2 * pos + 1 - parity, exp)
+    barrier = pltpu.get_barrier_semaphore()
+
+    def greet(slot, carry):
+        @pl.when(slot != mine)
+        def _():
+            pl.semaphore_signal(
+                barrier, inc=1, device_id=device(slot // n_exp, slot % n_exp), device_id_type=MESH
+            )
+
+        return carry
+
+    lax.fori_loop(0, slots, greet, 0)
+    pl.semaphore_signal(barrier, inc=1, device_id=partner, device_id_type=MESH)
+    pl.semaphore_wait(barrier, slots)
+
+    def sum_copy(step):
+        target = (exp + step) % n_exp
+        return remote(
+            part.at[target],
+            sums.at[step - 1],
+            sum_send.at[step - 1],
+            sum_recv.at[step - 1],
+            device(pos, target),
+        )
+
+    for step in range(1, n_exp):
+        sum_copy(step).start()
+    own_copy = pltpu.make_async_copy(own_weights, weights.at[0], w_sem.at[0])
+    own_copy.start()
+    pair_copy = remote(own_weights, weights.at[1], w_sem.at[1], w_sem.at[2], partner)
+    pair_copy.start()
+
+    total = residual[...].astype(jnp.float32) + part[exp].astype(jnp.float32)
+    for step in range(1, n_exp):
+        sum_copy(step).wait_recv()
+        total = total + sums[step - 1].astype(jnp.float32)
+    mixed_own = total.astype(jnp.bfloat16)
+    mixed[...] = mixed_own
+    mixed_f = mixed_own.astype(jnp.float32)
+    square = jnp.mean(mixed_f * mixed_f, axis=1, keepdims=True)
+    tokens[mine] = (mixed_f * lax.rsqrt(square + 1e-06) * gain[...]).astype(jnp.bfloat16)
+
+    def line_copy(block, way):
+        place = tokens.at[pos * n_exp + block]
+        return remote(
+            place,
+            place,
+            line_send.at[(way + 1) // 2, block],
+            line_recv.at[block],
+            device(pos, exp + way),
+        )
+
+    def ring_copy(block, hop, way, arrived):
+        back = hop if arrived else hop - 1
+        origin = ring_place((ring - way * back + n_pos) % n_pos)
+        place = tokens.at[origin * n_exp + block]
+        if hop == half:
+            columns = D // 2
+            place = place.at[:, pl.ds(0 if way > 0 else columns, columns)]
+        index = (way + 1) // 2
+        return remote(
+            place,
+            place,
+            ring_send.at[index, hop - 1, block],
+            ring_recv.at[index, hop - 1, block],
+            device(ring_place((ring + way + n_pos) % n_pos), exp),
+        )
+
+    def blocks_of(step, action):
+        if step == 0:
+            action(exp, 0)
+            return
+
+        @pl.when(exp >= step)
+        def _():
+            action(exp - step, 1)
+
+        @pl.when(exp + step < n_exp)
+        def _():
+            action(exp + step, -1)
+
+    def line_sends(block, way, act):
+        for out in (1, -1) if way == 0 else (way,):
+
+            @pl.when((exp + out >= 0) & (exp + out < n_exp))
+            def _():
+                act(line_copy(block, out))
+
+    def line_step(block, way):
+        if way != 0:
+            line_copy(block, way).wait_recv()
+        line_sends(block, way, lambda copy: copy.start())
+        for out in (1, -1):
+            ring_copy(block, 1, out, False).start()
+
+    def ring_step(hop):
+        def action(block, way):
+            for out in (1, -1):
+                ring_copy(block, hop, out, True).wait_recv()
+                if hop < half:
+                    ring_copy(block, hop + 1, out, False).start()
+
+        return action
+
+    tile = min(256, weights.shape[2])
+    tiles = weights.shape[2] // tile
+
+    def back_copy(place, index):
+        slot = place * n_exp + index
+        return remote(
+            hidden.at[slot],
+            ret.at[mine],
+            back_send.at[slot],
+            back_recv.at[mine],
+            device(place, index),
+        )
+
+    def back_local(slot):
+        return pltpu.make_async_copy(hidden.at[slot], ret.at[slot], back_recv.at[slot])
+
+    def compute(place):
+        rows = tokens[pl.ds(place * n_exp, n_exp)]
+        if tok_dev % 16:
+            rows = rows.astype(jnp.float32).reshape(n_exp * tok_dev, D).astype(jnp.bfloat16)
+        else:
+            rows = rows.reshape(n_exp * tok_dev, D)
+        for which in range(2):
+            for index in range(tiles):
+                units[:, index * tile : (index + 1) * tile] = jnp.dot(
+                    rows,
+                    weights[which, :, index * tile : (index + 1) * tile],
+                    preferred_element_type=jnp.float32,
+                )
+            gate, upper = units[:, :width], units[:, width:]
+            result = gate / (1.0 + jnp.exp(-gate)) * upper
+            side = parity if which == 0 else 1 - parity
+            for index in range(n_exp):
+                hidden[place * n_exp + index, side] = result[
+                    index * tok_dev : (index + 1) * tok_dev
+                ].astype(jnp.bfloat16)
+        for index in range(n_exp):
+            slot = place * n_exp + index
+
+            @pl.when(slot != mine)
+            def _():
+                back_copy(place, index).start()
+
+            @pl.when(slot == mine)
+            def _():
+                back_local(slot).start()
+
+    own_copy.wait()
+    for step in range(n_exp + half - 1):
+        if step < n_exp:
+            blocks_of(step, line_step)
+        if step == n_exp - 1:
+            pair_copy.wait()
+            compute(pos)
+        for hop in range(1, half):
+            if 0 <= step - hop < n_exp:
+                blocks_of(step - hop, ring_step(hop))
+    for hop in range(1, half):
+        for way in (1, -1):
+            compute(ring_place((ring + way * hop + n_pos) % n_pos))
+    for step in range(n_exp):
+        blocks_of(step, ring_step(half))
+    compute(ring_place((ring + half) % n_pos))
+
+    for step in range(1, n_exp):
+        sum_copy(step).wait_send()
+
+    def finish(block, way):
+        line_sends(block, way, lambda copy: copy.wait_send())
+        for hop in range(1, half + 1):
+            for out in (1, -1):
+                ring_copy(block, hop, out, False).wait_send()
+
+    for step in range(n_exp):
+        blocks_of(step, finish)
+
+    def collect(slot, carry):
+        @pl.when(slot != mine)
+        def _():
+            back_copy(slot // n_exp, slot % n_exp).wait_send()
+            remote(
+                hidden.at[slot],
+                ret.at[slot],
+                back_send.at[slot],
+                back_recv.at[slot],
+                device(slot // n_exp, slot % n_exp),
+            ).wait_recv()
+
+        @pl.when(slot == mine)
+        def _():
+            back_local(slot).wait()
+
+        return carry
+
+    lax.fori_loop(0, slots, collect, 0)
+
+
+def expert_layer(n_ctx, n_exp, part, residual, gain, own_weights):
+    n_pos = n_ctx // 2
+    slots = n_pos * n_exp
+    tok_dev = residual.shape[0]
+    columns = own_weights.shape[1]
+    width = columns // 2
+    half = n_pos // 2
+    dma = pltpu.SemaphoreType.DMA
+    vmem = pl.BlockSpec(memory_space=pltpu.VMEM)
+    return pl.pallas_call(
+        functools.partial(expert_kernel, n_pos, n_exp),
+        out_shape=(
+            jax.ShapeDtypeStruct((tok_dev, D), jnp.bfloat16),
+            jax.ShapeDtypeStruct((slots, 2, tok_dev, width), jnp.bfloat16),
+        ),
+        in_specs=[vmem, vmem, vmem, pl.BlockSpec(memory_space=pl.ANY)],
+        out_specs=(vmem, vmem),
+        scratch_shapes=[
+            pltpu.VMEM((slots, tok_dev, D), jnp.bfloat16),
+            pltpu.VMEM((n_exp * tok_dev, columns), jnp.float32),
+            pltpu.VMEM((slots, 2, tok_dev, width), jnp.bfloat16),
+            pltpu.VMEM((n_exp - 1, tok_dev, D), jnp.bfloat16),
+            pltpu.VMEM((2, D, columns), jnp.bfloat16),
+            dma((3,)),
+            dma((n_exp - 1,)),
+            dma((n_exp - 1,)),
+            dma((2, n_exp)),
+            dma((n_exp,)),
+            dma((2, half, n_exp)),
+            dma((2, half, n_exp)),
+            dma((slots,)),
+            dma((slots,)),
+        ],
+        compiler_params=pltpu.CompilerParams(
+            collective_id=0, has_side_effects=True, vmem_limit_bytes=48 * 1024 * 1024
+        ),
+        cost_estimate=pl.CostEstimate(
+            flops=4 * slots * tok_dev * D * columns, bytes_accessed=1 << 23, transcendentals=0
+        ),
+    )(part, residual, gain, own_weights)
+
+
 def shards(
+    n_ctx,
+    n_exp,
     residual,
     queries,
     keys,
@@ -91,35 +394,19 @@
     attn = (accum / total[:, :, None]).astype(jnp.bfloat16)
     attn = jnp.transpose(attn, (1, 0, 2)).reshape(tok_rows, per_device * HD)
     tok_dev = residual.shape[0]
-    head_total = lax.psum_scatter(
-        jnp.dot(attn, out_proj, preferred_element_type=jnp.float32).astype(jnp.bfloat16),
-        "exp",
-        scatter_dimension=0,
-        tiled=True,
-    ).astype(jnp.float32)
-    mixed = (residual.astype(jnp.float32) + head_total).astype(jnp.bfloat16)
-    mixed_f = mixed.astype(jnp.float32)
-    square = jnp.mean(mixed_f * mixed_f, axis=1, keepdims=True)
-    normed = (mixed_f * lax.rsqrt(square + 1e-06) * norm_gain[None, :]).astype(jnp.bfloat16)
-    every = lax.all_gather(normed, ("ctx", "exp"), axis=0, tiled=True)
+    part = jnp.dot(attn, out_proj, preferred_element_type=jnp.float32).astype(jnp.bfloat16)
     experts, _, width = expert_gate.shape
-    devices = every.shape[0] // tok_dev
-    weights = jnp.transpose(jnp.stack((expert_gate, expert_up)), (2, 0, 1, 3))
-    units = jnp.dot(
-        every, weights.reshape(D, 2 * experts * width), preferred_element_type=jnp.float32
+    own_weights = jnp.transpose(jnp.stack((expert_gate, expert_up)), (2, 0, 1, 3))
+    mixed, returned = expert_layer(
+        n_ctx,
+        n_exp,
+        part.reshape(n_exp, tok_dev, D),
+        residual,
+        norm_gain[None, :],
+        own_weights.reshape(D, 2 * experts * width),
     )
-    gate, upper = units[:, : experts * width], units[:, experts * width :]
-    hidden = (jax.nn.silu(gate) * upper).astype(jnp.bfloat16)
-    returned = lax.all_to_all(
-        hidden.reshape(devices, tok_dev, experts * width),
-        ("ctx", "exp"),
-        split_axis=0,
-        concat_axis=0,
-        tiled=True,
-    )
-    n_exp = EXPERTS // experts
-    returned = returned.reshape(devices // n_exp, n_exp, tok_dev, experts, width)
-    returned = jnp.transpose(returned, (2, 1, 3, 0, 4)).reshape(tok_dev * EXPERTS, FE)
+    returned = returned.reshape(n_ctx // 2, n_exp, 2, tok_dev, experts, width)
+    returned = jnp.transpose(returned, (3, 1, 4, 0, 2, 5)).reshape(tok_dev * EXPERTS, FE)
     target = jnp.arange(tok_dev, dtype=jnp.int32)[:, None] * EXPERTS + expert_ids
     picked = jnp.take(returned, target.reshape(-1), axis=0).astype(jnp.float32)
     routed = (picked * route_weight.reshape(-1)[:, None]).astype(jnp.bfloat16)
@@ -141,4 +428,5 @@
         P(("ctx", "exp"), None),
     )
     out_specs = (P(("ctx", "exp"), None), P(("ctx", "exp"), None, None))
-    return jax.shard_map(shards, mesh=mesh, in_specs=in_specs, out_specs=out_specs, check_vma=False)
+    body = functools.partial(shards, mesh.shape["ctx"], mesh.shape["exp"])
+    return jax.shard_map(body, mesh=mesh, in_specs=in_specs, out_specs=out_specs, check_vma=False)

time: 183 us -> 117 us (0.64)
  waiting for transfers between devices: 119 us -> 0 us
  Pallas kernels: 0 us -> 76.8 us
  between operations: 14.3 us -> 0.84 us
  matrix products: 14.9 us -> 2.99 us
  local copies, waits for them, and re-layouts: 6.78 us -> 17.4 us
  other arithmetic: 12.1 us -> 6.77 us
  starting transfers between devices: 3.45 us -> 0 us
    pallas_call x0 -> x1, Pallas kernels: none -> 76.8 us  [expert_layer(): pl.pallas_call(functools.partial(expert_kernel, n_pos, n_exp), out_shape=...]
    all_gather x1 -> x0, waiting for transfers between devices: 72 us -> none  [shards(): every = lax.all_gather(normed, ('ctx', 'exp'), axis=0, tiled=True)]
    reduce_scatter x1 -> x0, waiting for transfers between devices: 27.6 us -> none  [shards(): lax.psum_scatter(jnp.dot(attn, out_proj, preferred_element_type=jnp.float...]
    all_to_all x1 -> x0, waiting for transfers between devices: 19 us -> none  [shards(): lax.all_to_all(hidden.reshape(devices, tok_dev, experts * width), ('ctx',...]
    dot_general x1 -> x0, matrix products: 11 us -> none  [shards(): jnp.dot(every, weights.reshape(D, 2 * experts * width), preferred_element...]
    reshape x3, local copies, waits for them, and re-layouts: 2.71 us -> 10.2 us  [the longest x1 8.66 us: shards(): own_weights.reshape(D, 2 * experts * width)]
    all_to_all x1 -> x0, starting transfers between devices: 3.37 us -> none  [shards(): lax.all_to_all(hidden.reshape(devices, tok_dev, experts * width), ('ctx',...]
    convert_element_type x2 -> x0, other arithmetic: 2.16 us -> none  [the longest x1 1.33 us: shards(): hidden = (jax.nn.silu(gate) * upper).astype(jnp.bfloat16)]
  transfers between devices with their start and end apart: 3 -> 0, of which waited for: 3 -> 0; matrix products, arithmetic and copies ran while one was open for 3% -> 0% of each run, Pallas kernels for 0% -> 0%
where the time goes in v2:
time: 117 us; the launch traced here: 116 us
  Pallas kernels  76.8 us (66%)
  local copies, waits for them, and re-layouts  17.4 us (15%)
  blocking collectives  11.3 us (10%)
  other arithmetic  6.77 us (6%)
  matrix products  2.99 us (3%)
    pallas_call x1, Pallas kernels, expert_layer(): pl.pallas_call(functools.partial(expert_kernel, n_pos, n_exp), out_shape=...  76.8 us
    all_gather x1, blocking collectives, shards(): lax.all_gather(jnp.concatenate((own_keys, own_values), axis=1), 'ctx', ax...  11.3 us
    reshape x1, local copies, waits for them, and re-layouts, shards(): own_weights.reshape(D, 2 * experts * width)  8.66 us
    unnamed x20, local copies, waits for them, and re-layouts  3.38 us
    another operation x1, other arithmetic, shards(): jnp.stack((expert_gate, expert_up))  3.19 us

profile of v2, /device:TPU:0, one launch (start us, length us, event | category | flops | bytes accessed | tf_op | source)
XLA Modules:
  0.0 116.1 jit_solution(13463019725454982733)
XLA Ops:
  0.6 0.0 copy-start
  0.7 0.8 constant_dynamic-slice_fusion
  1.5 11.3 %all_gather.3 = bf16[1024,256]{1,0:T(8,128)(2,1)S(1)} all-gather(bf16[128,256]{1,0:T(8,128)(2,1)S(1)} %pad_maximum_fusion.1), channel_id=1, replica_groups=mesh['ctx'=8,'exp'=4] {'ctx'}, dimensions={0}, use_global_device_ids=true | all-gather | bytes 589824 | tf_op jit(solution)/shard_map/all_gather | solution.py:360
  12.8 0.7 select_reduce_fusion.1
  13.6 0.7 select_reduce_fusion
  14.3 0.2 broadcast_compare_fusion
  14.6 0.0 copy-done
  14.6 0.0 slice-start
  14.6 0.8 fusion
  15.4 0.0 slice-start.1
  15.4 0.9 fusion.3
  16.3 0.9 fusion.17
  17.2 0.0 slice-done
  17.2 1.0 slice-done.1
  18.2 0.0 copy-start.3
  18.2 0.0 copy-start.4
  18.2 1.3 %convolution_convert_fusion = bf16[128,4096]{1,0:T(8,128)(2,1)S(1)} fusion(bf16[128,1024]{0,1:T(8,128)(2,1)S(1)} %bitcast.79, bf16[1024,4096]{1,0:T(8,128)(2,1)S(1)} %bitcast.75), kind=kOutput, calls=%fused_computation.2 | convolution fusion | flops 1074266112 | bytes 9699328 | tf_op jit(solution)/shard_map/dot_general | solution.py:397
  19.5 0.6 copy-done.3
  20.1 1.0 copy-done.4
  21.1 3.2 %pad_maximum_fusion = bf16[2,4,4096,96]{2,3,1,0:T(8,128)(2,1)} fusion(bf16[1,4,4096,96]{2,3,1,0:T(8,128)(2,1)S(1)} %bitcast.77, bf16[1,4,4096,96]{2,3,1,0:T(8,128)(2,1)S(1)} %bitcast.78), kind=kLoop, calls=%fused_computation.1 | loop fusion | flops 3145728 | bytes 12582912 | tf_op jit(solution)/shard_map/stack | solution.py:399
  24.3 0.0 copy-start.1
  24.3 0.0 copy-start.2
  24.3 8.7 %copy.31.own_weights = bf16[4096,768]{1,0:T(8,128)(2,1)} copy(bf16[4096,768]{0,1:T(8,128)(2,1)} %bitcast.73) | data formatting | bytes 12582912 | tf_op jit(solution)/shard_map/reshape | solution.py:406
  32.9 0.0 copy-done.1
  32.9 0.0 copy-done.2
  32.9 76.8 %shard_map.122 = (bf16[32,4096]{1,0:T(8,128)(2,1)S(1)}, bf16[16,2,32,384]{3,2,1,0:T(8,128)(2,1)S(1)}) custom-call(bf16[4,32,4096]{2,1,0:T(8,128)(2,1)S(1)} %bitcast.71, bf16[32,4096]{1,0:T(8,128)(2,1)S(1)} %copy-done.1, f32[1,4096]{1,0:T(1,128)S(1)} %bitcast.72, bf16[4096,768]{1,0:T(8,128)(2,1)} %copy.31.own_weights), custom_call_target="tpu_custom_call" | custom-call | flops 6442450944 | bytes 8388608 | tf_op jit(solution)/shard_map/pallas_call | solution.py:294
  109.7 0.0 copy-start.6
  109.8 0.6 reshape.190
  110.4 0.0 copy-start.5
  110.4 1.6 %copy.33 = bf16[32,4,4,4,2,96]{5,4,3,2,1,0:T(2,128)(2,1)S(1)} copy(bf16[32,4,4,4,2,96]{5,2,0,4,1,3:T(4,128)(2,1)S(1)} %bitcast.76) | data formatting | bytes 1572864 | tf_op jit(solution)/shard_map/transpose | solution.py:409
  112.0 0.9 reshape.191
  112.9 0.0 copy-done.6
  112.9 0.1 copy.34
  113.0 0.1 reshape.192
  113.1 1.2 %gather_fusion = bf16[256,768]{1,0:T(8,128)(2,1)S(1)} fusion(bf16[512,768]{1,0:T(8,128)(2,1)S(1)} %reshape.191, s32[1024]{0:T(1024)S(1)} %pad_clamp_fusion), kind=kCustom, calls=%fused_computation | custom fusion | bytes 787456 | tf_op jit(solution)/shard_map/jit(_take)/gather | solution.py:411
  114.3 0.1 copy.32
  114.4 0.0 copy-done.5
  114.4 0.1 copy.35
  114.5 0.9 multiply_convert_fusion
  115.4 0.7 copy.47
  (12 shorter events, 0.1 us)
Async XLA Ops:
  0.6 13.9 %copy-start = (bf16[128,1024]{1,0:T(8,128)(2,1)S(1)}, bf16[128,1024]{1,0:T(8,128)(2,1)}, u32[]{:S(2)}) copy-start(bf16[128,1024]{1,0:T(8,128)(2,1)} %param.12) | copy-start | bytes 786436
  14.6 2.6 %slice-start = ((s8[8388608]{0:T(1024)(128)(4,1)}), s8[4194304]{0:T(1024)(128)(4,1)S(1)}, s32[]{:S(2)}) async-start(s8[8388608]{0:T(1024)(128)(4,1)} %bitcast.74), calls=%async_computation | async-start | bytes 8388608
  15.4 2.9 %slice-start.1 = ((s8[8388608]{0:T(1024)(128)(4,1)}), s8[4194304]{0:T(1024)(128)(4,1)S(1)}, s32[]{:S(2)}) async-start(s8[8388608]{0:T(1024)(128)(4,1)} %bitcast.74), calls=%async_computation.1 | async-start | bytes 8388608
  18.2 1.9 %copy-start.3 = (bf16[4,4096,96]{1,2,0:T(8,128)(2,1)S(1)}, bf16[4,4096,96]{1,2,0:T(8,128)(2,1)}, u32[]{:S(2)}) copy-start(bf16[4,4096,96]{1,2,0:T(8,128)(2,1)} %param.19) | copy-start | bytes 9437188
  18.2 2.8 %copy-start.4 = (bf16[4,4096,96]{1,2,0:T(8,128)(2,1)S(1)}, bf16[4,4096,96]{1,2,0:T(8,128)(2,1)}, u32[]{:S(2)}) copy-start(bf16[4,4096,96]{1,2,0:T(8,128)(2,1)} %param.18) | copy-start | bytes 9437188
  24.3 8.7 %copy-start.1 = (bf16[32,4096]{1,0:T(8,128)(2,1)S(1)}, bf16[32,4096]{1,0:T(8,128)(2,1)}, u32[]{:S(2)}) copy-start(bf16[32,4096]{1,0:T(8,128)(2,1)} %residual.1) | copy-start | bytes 786436
  24.3 8.7 %copy-start.2 = (f32[4096]{0:T(1024)S(1)}, f32[4096]{0:T(1024)}, u32[]{:S(2)}) copy-start(f32[4096]{0:T(1024)} %param.17) | copy-start | bytes 49156
  109.7 3.2 %copy-start.6 = (s32[32,8]{0,1:T(8,128)S(1)}, s32[32,8]{0,1:T(8,128)}, u32[]{:S(2)}) copy-start(s32[32,8]{0,1:T(8,128)} %param.20) | copy-start | bytes 3076
  110.4 4.0 %copy-start.5 = (f32[32,8]{0,1:T(8,128)S(1)}, f32[32,8]{0,1:T(8,128)}, u32[]{:S(2)}) copy-start(f32[32,8]{0,1:T(8,128)} %param.21) | copy-start | bytes 3076

commit v3 on v2

--- a/solution.py
+++ b/solution.py
@@ -26,6 +26,7 @@
     return base * CH + rows % CH
 
 
+CHUNKS = 2
 MESH = pl.DeviceIdType.MESH
 
 
@@ -40,10 +41,12 @@
     part,
     residual,
     gain,
-    own_weights,
+    own_gate,
+    own_upper,
     mixed,
     ret,
     tokens,
+    normed,
     units,
     hidden,
     sums,
@@ -66,6 +69,8 @@
     mine = pos * n_exp + exp
     tok_dev = residual.shape[0]
     width = hidden.shape[3]
+    padded = weights.shape[1] // 2
+    chunk = D // CHUNKS
 
     def device(place, index):
         return (2 * place + parity, index)
@@ -96,56 +101,77 @@
     pl.semaphore_signal(barrier, inc=1, device_id=partner, device_id_type=MESH)
     pl.semaphore_wait(barrier, slots)
 
-    def sum_copy(step):
+    def columns_of(piece):
+        return pl.ds(piece * chunk, chunk)
+
+    def sum_copy(step, piece):
         target = (exp + step) % n_exp
         return remote(
-            part.at[target],
-            sums.at[step - 1],
-            sum_send.at[step - 1],
-            sum_recv.at[step - 1],
+            part.at[target, :, columns_of(piece)],
+            sums.at[step - 1, :, columns_of(piece)],
+            sum_send.at[step - 1, piece],
+            sum_recv.at[step - 1, piece],
             device(pos, target),
         )
 
-    for step in range(1, n_exp):
-        sum_copy(step).start()
-    own_copy = pltpu.make_async_copy(own_weights, weights.at[0], w_sem.at[0])
-    own_copy.start()
-    pair_copy = remote(own_weights, weights.at[1], w_sem.at[1], w_sem.at[2], partner)
-    pair_copy.start()
-
-    total = residual[...].astype(jnp.float32) + part[exp].astype(jnp.float32)
-    for step in range(1, n_exp):
-        sum_copy(step).wait_recv()
-        total = total + sums[step - 1].astype(jnp.float32)
-    mixed_own = total.astype(jnp.bfloat16)
-    mixed[...] = mixed_own
-    mixed_f = mixed_own.astype(jnp.float32)
-    square = jnp.mean(mixed_f * mixed_f, axis=1, keepdims=True)
-    tokens[mine] = (mixed_f * lax.rsqrt(square + 1e-06) * gain[...]).astype(jnp.bfloat16)
-
-    def line_copy(block, way):
-        place = tokens.at[pos * n_exp + block]
+    def own_copy(which):
+        return pltpu.make_async_copy(
+            (own_gate, own_upper)[which],
+            weights.at[0, pl.ds(which * padded, width)],
+            w_sem.at[0, which],
+        )
+
+    def pair_copy(which):
+        return remote(
+            (own_gate, own_upper)[which],
+            weights.at[1, pl.ds(which * padded, width)],
+            w_sem.at[1, which],
+            w_sem.at[2, which],
+            partner,
+        )
+
+    for piece in range(CHUNKS):
+        for step in range(1, n_exp):
+            sum_copy(step, piece).start()
+    for which in range(2):
+        own_copy(which).start()
+        pair_copy(which).start()
+
+    def add_up(piece):
+        columns = slice(piece * chunk, (piece + 1) * chunk)
+        total = residual[:, columns].astype(jnp.float32)
+        total = total + part[exp, :, columns].astype(jnp.float32)
+        for step in range(1, n_exp):
+            sum_copy(step, piece).wait_recv()
+            total = total + sums[step - 1, :, columns].astype(jnp.float32)
+        total = total.astype(jnp.bfloat16)
+        mixed[:, columns] = total
+        tokens[mine, :, columns] = total
+
+    def line_copy(block, way, piece):
+        place = tokens.at[pos * n_exp + block, :, columns_of(piece)]
         return remote(
             place,
             place,
-            line_send.at[(way + 1) // 2, block],
-            line_recv.at[block],
+            line_send.at[(way + 1) // 2, block, piece],
+            line_recv.at[block, piece],
             device(pos, exp + way),
         )
 
-    def ring_copy(block, hop, way, arrived):
+    def ring_copy(block, hop, way, arrived, piece):
         back = hop if arrived else hop - 1
         origin = ring_place((ring - way * back + n_pos) % n_pos)
-        place = tokens.at[origin * n_exp + block]
+        first, columns = piece * chunk, chunk
         if hop == half:
-            columns = D // 2
-            place = place.at[:, pl.ds(0 if way > 0 else columns, columns)]
+            columns = chunk // 2
+            first += 0 if way > 0 else columns
+        place = tokens.at[origin * n_exp + block, :, pl.ds(first, columns)]
         index = (way + 1) // 2
         return remote(
             place,
             place,
-            ring_send.at[index, hop - 1, block],
-            ring_recv.at[index, hop - 1, block],
+            ring_send.at[index, hop - 1, block, piece],
+            ring_recv.at[index, hop - 1, block, piece],
             device(ring_place((ring + way + n_pos) % n_pos), exp),
         )
 
@@ -162,31 +188,34 @@
         def _():
             action(exp + step, -1)
 
-    def line_sends(block, way, act):
+    def line_sends(block, way, piece, act):
         for out in (1, -1) if way == 0 else (way,):
 
             @pl.when((exp + out >= 0) & (exp + out < n_exp))
             def _():
-                act(line_copy(block, out))
-
-    def line_step(block, way):
-        if way != 0:
-            line_copy(block, way).wait_recv()
-        line_sends(block, way, lambda copy: copy.start())
-        for out in (1, -1):
-            ring_copy(block, 1, out, False).start()
-
-    def ring_step(hop):
+                act(line_copy(block, out, piece))
+
+    def line_step(piece):
+        def action(block, way):
+            if way != 0:
+                line_copy(block, way, piece).wait_recv()
+            line_sends(block, way, piece, lambda copy: copy.start())
+            for out in (1, -1):
+                ring_copy(block, 1, out, False, piece).start()
+
+        return action
+
+    def ring_step(hop, piece):
         def action(block, way):
             for out in (1, -1):
-                ring_copy(block, hop, out, True).wait_recv()
+                ring_copy(block, hop, out, True, piece).wait_recv()
                 if hop < half:
-                    ring_copy(block, hop + 1, out, False).start()
+                    ring_copy(block, hop + 1, out, False, piece).start()
 
         return action
 
-    tile = min(256, weights.shape[2])
-    tiles = weights.shape[2] // tile
+    tile = min(256, 2 * padded)
+    tiles = 2 * padded // tile
 
     def back_copy(place, index):
         slot = place * n_exp + index
@@ -202,19 +231,24 @@
         return pltpu.make_async_copy(hidden.at[slot], ret.at[slot], back_recv.at[slot])
 
     def compute(place):
-        rows = tokens[pl.ds(place * n_exp, n_exp)]
+        for index in range(n_exp):
+            row = tokens[place * n_exp + index].astype(jnp.float32)
+            square = jnp.mean(row * row, axis=1, keepdims=True)
+            normed[index] = (row * lax.rsqrt(square + 1e-06) * gain[...]).astype(jnp.bfloat16)
+        rows = normed[...]
         if tok_dev % 16:
             rows = rows.astype(jnp.float32).reshape(n_exp * tok_dev, D).astype(jnp.bfloat16)
         else:
             rows = rows.reshape(n_exp * tok_dev, D)
         for which in range(2):
             for index in range(tiles):
-                units[:, index * tile : (index + 1) * tile] = jnp.dot(
+                units[:, index * tile : (index + 1) * tile] = lax.dot_general(
                     rows,
-                    weights[which, :, index * tile : (index + 1) * tile],
+                    weights[which, index * tile : (index + 1) * tile],
+                    (((1,), (1,)), ((), ())),
                     preferred_element_type=jnp.float32,
                 )
-            gate, upper = units[:, :width], units[:, width:]
+            gate, upper = units[:, :width], units[:, padded : padded + width]
             result = gate / (1.0 + jnp.exp(-gate)) * upper
             side = parity if which == 0 else 1 - parity
             for index in range(n_exp):
@@ -232,34 +266,44 @@
             def _():
                 back_local(slot).start()
 
-    own_copy.wait()
-    for step in range(n_exp + half - 1):
-        if step < n_exp:
-            blocks_of(step, line_step)
-        if step == n_exp - 1:
-            pair_copy.wait()
-            compute(pos)
-        for hop in range(1, half):
-            if 0 <= step - hop < n_exp:
-                blocks_of(step - hop, ring_step(hop))
+    lag = 2
+    for time in range(n_exp + half - 1 + lag * (CHUNKS - 1)):
+        for piece in reversed(range(CHUNKS)):
+            step = time - lag * piece
+            if step == 0:
+                add_up(piece)
+            if 0 <= step < n_exp:
+                blocks_of(step, line_step(piece))
+            if step == n_exp - 1 and piece == CHUNKS - 1:
+                for which in range(2):
+                    own_copy(which).wait()
+                    pair_copy(which).wait()
+                compute(pos)
+        for piece in range(CHUNKS):
+            for hop in range(1, half):
+                step = time - lag * piece - hop
+                if 0 <= step < n_exp:
+                    blocks_of(step, ring_step(hop, piece))
     for hop in range(1, half):
         for way in (1, -1):
             compute(ring_place((ring + way * hop + n_pos) % n_pos))
-    for step in range(n_exp):
-        blocks_of(step, ring_step(half))
+    for piece in range(CHUNKS):
+        for step in range(n_exp):
+            blocks_of(step, ring_step(half, piece))
     compute(ring_place((ring + half) % n_pos))
 
-    for step in range(1, n_exp):
-        sum_copy(step).wait_send()
-
-    def finish(block, way):
-        line_sends(block, way, lambda copy: copy.wait_send())
-        for hop in range(1, half + 1):
-            for out in (1, -1):
-                ring_copy(block, hop, out, False).wait_send()
-
-    for step in range(n_exp):
-        blocks_of(step, finish)
+    for piece in range(CHUNKS):
+        for step in range(1, n_exp):
+            sum_copy(step, piece).wait_send()
+
+        def finish(block, way):
+            line_sends(block, way, piece, lambda copy: copy.wait_send())
+            for hop in range(1, half + 1):
+                for out in (1, -1):
+                    ring_copy(block, hop, out, False, piece).wait_send()
+
+        for step in range(n_exp):
+            blocks_of(step, finish)
 
     def collect(slot, carry):
         @pl.when(slot != mine)
@@ -282,12 +326,12 @@
     lax.fori_loop(0, slots, collect, 0)
 
 
-def expert_layer(n_ctx, n_exp, part, residual, gain, own_weights):
+def expert_layer(n_ctx, n_exp, part, residual, gain, own_gate, own_upper):
     n_pos = n_ctx // 2
     slots = n_pos * n_exp
     tok_dev = residual.shape[0]
-    columns = own_weights.shape[1]
-    width = columns // 2
+    width = own_gate.shape[0]
+    padded = -(-width // 16) * 16
     half = n_pos // 2
     dma = pltpu.SemaphoreType.DMA
     vmem = pl.BlockSpec(memory_space=pltpu.VMEM)
@@ -297,21 +341,22 @@
             jax.ShapeDtypeStruct((tok_dev, D), jnp.bfloat16),
             jax.ShapeDtypeStruct((slots, 2, tok_dev, width), jnp.bfloat16),
         ),
-        in_specs=[vmem, vmem, vmem, pl.BlockSpec(memory_space=pl.ANY)],
+        in_specs=[vmem, vmem, vmem] + [pl.BlockSpec(memory_space=pl.ANY)] * 2,
         out_specs=(vmem, vmem),
         scratch_shapes=[
             pltpu.VMEM((slots, tok_dev, D), jnp.bfloat16),
-            pltpu.VMEM((n_exp * tok_dev, columns), jnp.float32),
+            pltpu.VMEM((n_exp, tok_dev, D), jnp.bfloat16),
+            pltpu.VMEM((n_exp * tok_dev, 2 * padded), jnp.float32),
             pltpu.VMEM((slots, 2, tok_dev, width), jnp.bfloat16),
             pltpu.VMEM((n_exp - 1, tok_dev, D), jnp.bfloat16),
-            pltpu.VMEM((2, D, columns), jnp.bfloat16),
-            dma((3,)),
-            dma((n_exp - 1,)),
-            dma((n_exp - 1,)),
-            dma((2, n_exp)),
-            dma((n_exp,)),
-            dma((2, half, n_exp)),
-            dma((2, half, n_exp)),
+            pltpu.VMEM((2, 2 * padded, D), jnp.bfloat16),
+            dma((3, 2)),
+            dma((n_exp - 1, CHUNKS)),
+            dma((n_exp - 1, CHUNKS)),
+            dma((2, n_exp, CHUNKS)),
+            dma((n_exp, CHUNKS)),
+            dma((2, half, n_exp, CHUNKS)),
+            dma((2, half, n_exp, CHUNKS)),
             dma((slots,)),
             dma((slots,)),
         ],
@@ -319,9 +364,9 @@
             collective_id=0, has_side_effects=True, vmem_limit_bytes=48 * 1024 * 1024
         ),
         cost_estimate=pl.CostEstimate(
-            flops=4 * slots * tok_dev * D * columns, bytes_accessed=1 << 23, transcendentals=0
+            flops=8 * slots * tok_dev * D * width, bytes_accessed=1 << 23, transcendentals=0
         ),
-    )(part, residual, gain, own_weights)
+    )(part, residual, gain, own_gate, own_upper)
 
 
 def shards(
@@ -396,14 +441,14 @@
     tok_dev = residual.shape[0]
     part = jnp.dot(attn, out_proj, preferred_element_type=jnp.float32).astype(jnp.bfloat16)
     experts, _, width = expert_gate.shape
-    own_weights = jnp.transpose(jnp.stack((expert_gate, expert_up)), (2, 0, 1, 3))
     mixed, returned = expert_layer(
         n_ctx,
         n_exp,
         part.reshape(n_exp, tok_dev, D),
         residual,
         norm_gain[None, :],
-        own_weights.reshape(D, 2 * experts * width),
+        jnp.transpose(expert_gate, (0, 2, 1)).reshape(experts * width, D),
+        jnp.transpose(expert_up, (0, 2, 1)).reshape(experts * width, D),
     )
     returned = returned.reshape(n_ctx // 2, n_exp, 2, tok_dev, experts, width)
     returned = jnp.transpose(returned, (3, 1, 4, 0, 2, 5)).reshape(tok_dev * EXPERTS, FE)

time: 117 us -> 108 us (0.923)
  local copies, waits for them, and re-layouts: 17.4 us -> 7.81 us
  Pallas kernels: 76.8 us -> 81.4 us
  other arithmetic: 6.77 us -> 3.58 us
    reshape x1 -> x0, local copies, waits for them, and re-layouts: 8.66 us -> none  [shards(): own_weights.reshape(D, 2 * experts * width)]
    pallas_call x1, Pallas kernels: 76.8 us -> 81.4 us  [expert_layer(): pl.pallas_call(functools.partial(expert_kernel, n_pos, n_exp), out_shape=...]
    another operation x1 -> x0, other arithmetic: 3.19 us -> none  [shards(): jnp.stack((expert_gate, expert_up))]
    unnamed x20 -> x18, local copies, waits for them, and re-layouts: 3.38 us -> 2.43 us
where the time goes in v3:
time: 108 us
  Pallas kernels  81.4 us (75%)
  blocking collectives  11.3 us (10%)
  local copies, waits for them, and re-layouts  7.81 us (7%)
  other arithmetic  3.58 us (3%)
  matrix products  2.99 us (3%)
    pallas_call x1, Pallas kernels, expert_layer(): pl.pallas_call(functools.partial(expert_kernel, n_pos, n_exp), out_shape=...  81.4 us
    all_gather x1, blocking collectives, shards(): lax.all_gather(jnp.concatenate((own_keys, own_values), axis=1), 'ctx', ax...  11.3 us
    unnamed x18, local copies, waits for them, and re-layouts  2.43 us

profile of v3, /device:TPU:0, one launch (start us, length us, event | category | flops | bytes accessed | tf_op | source)
XLA Modules:
  0.0 107.9 jit_solution(4002812826020059887)
XLA Ops:
  0.6 0.0 copy-start
  0.7 0.8 constant_dynamic-slice_fusion
  1.5 11.3 %all_gather.3 = bf16[1024,256]{1,0:T(8,128)(2,1)S(1)} all-gather(bf16[128,256]{1,0:T(8,128)(2,1)S(1)} %pad_maximum_fusion), channel_id=1, replica_groups=mesh['ctx'=8,'exp'=4] {'ctx'}, dimensions={0}, use_global_device_ids=true | all-gather | bytes 589824 | tf_op jit(solution)/shard_map/all_gather | solution.py:405
  12.8 0.7 select_reduce_fusion.1
  13.6 0.7 select_reduce_fusion
  14.3 0.2 broadcast_compare_fusion
  14.6 0.0 copy-done
  14.6 0.0 slice-start
  14.6 0.8 fusion
  15.4 0.0 slice-start.1
  15.4 0.9 fusion.3
  16.3 0.9 fusion.17
  17.2 0.0 slice-done
  17.2 1.0 slice-done.1
  18.2 0.0 copy-start.1
  18.2 0.0 copy-start.2
  18.2 0.0 copy-start.3
  18.2 1.3 %convolution_convert_fusion = bf16[128,4096]{1,0:T(8,128)(2,1)S(1)} fusion(bf16[128,1024]{0,1:T(8,128)(2,1)S(1)} %bitcast.78, bf16[1024,4096]{1,0:T(8,128)(2,1)S(1)} %bitcast.76), kind=kOutput, calls=%fused_computation.1 | convolution fusion | flops 1074266112 | bytes 9699328 | tf_op jit(solution)/shard_map/dot_general | solution.py:442
  19.5 0.6 copy-done.1
  20.1 0.0 copy-done.2
  20.1 0.0 copy-done.3
  20.1 81.4 %shard_map.122 = (bf16[32,4096]{1,0:T(8,128)(2,1)S(1)}, bf16[16,2,32,384]{3,2,1,0:T(8,128)(2,1)S(1)}) custom-call(bf16[4,32,4096]{2,1,0:T(8,128)(2,1)S(1)} %bitcast.72, bf16[32,4096]{1,0:T(8,128)(2,1)S(1)} %copy-done.2, f32[1,4096]{1,0:T(1,128)S(1)} %bitcast.74, bf16[384,4096]{1,0:T(8,128)(2,1)S(1)} %bitcast.73, bf16[384,4096]{1,0:T(8,128)(2,1)} %bitcast.80), custom_call_target="tpu_custom_call" | custom-call | flops 6442450944 | bytes 8388608 | tf_op jit(solution)/shard_map/pallas_call | solution.py:338
  101.6 0.0 copy-start.5
  101.6 0.6 reshape.194
  102.2 0.0 copy-start.4
  102.2 1.6 %copy.30 = bf16[32,4,4,4,2,96]{5,4,3,2,1,0:T(2,128)(2,1)S(1)} copy(bf16[32,4,4,4,2,96]{5,2,0,4,1,3:T(4,128)(2,1)S(1)} %bitcast.77) | data formatting | bytes 1572864 | tf_op jit(solution)/shard_map/transpose | solution.py:454
  103.8 0.9 reshape.195
  104.7 0.0 copy-done.5
  104.7 0.1 copy.31
  104.8 0.1 reshape.196
  104.9 1.2 %gather_fusion = bf16[256,768]{1,0:T(8,128)(2,1)S(1)} fusion(bf16[512,768]{1,0:T(8,128)(2,1)S(1)} %reshape.195, s32[1024]{0:T(1024)S(1)} %pad_clamp_fusion), kind=kCustom, calls=%fused_computation | custom fusion | bytes 787456 | tf_op jit(solution)/shard_map/jit(_take)/gather | solution.py:456
  106.1 0.1 copy.29
  106.2 0.0 copy-done.4
  106.2 0.1 copy.32
  106.3 0.9 multiply_convert_fusion
  107.2 0.7 copy.44
  (12 shorter events, 0.1 us)
Async XLA Ops:
  0.6 13.9 %copy-start = (bf16[128,1024]{1,0:T(8,128)(2,1)S(1)}, bf16[128,1024]{1,0:T(8,128)(2,1)}, u32[]{:S(2)}) copy-start(bf16[128,1024]{1,0:T(8,128)(2,1)} %param.12) | copy-start | bytes 786436
  14.6 2.6 %slice-start = ((s8[8388608]{0:T(1024)(128)(4,1)}), s8[4194304]{0:T(1024)(128)(4,1)S(1)}, s32[]{:S(2)}) async-start(s8[8388608]{0:T(1024)(128)(4,1)} %bitcast.75), calls=%async_computation | async-start | bytes 8388608
  15.4 2.9 %slice-start.1 = ((s8[8388608]{0:T(1024)(128)(4,1)}), s8[4194304]{0:T(1024)(128)(4,1)S(1)}, s32[]{:S(2)}) async-start(s8[8388608]{0:T(1024)(128)(4,1)} %bitcast.75), calls=%async_computation.1 | async-start | bytes 8388608
  18.2 1.9 %copy-start.1 = (bf16[4,4096,96]{1,2,0:T(8,128)(2,1)S(1)}, bf16[4,4096,96]{1,2,0:T(8,128)(2,1)}, u32[]{:S(2)}) copy-start(bf16[4,4096,96]{1,2,0:T(8,128)(2,1)} %param.18) | copy-start | bytes 9437188
  18.2 1.9 %copy-start.2 = (bf16[32,4096]{1,0:T(8,128)(2,1)S(1)}, bf16[32,4096]{1,0:T(8,128)(2,1)}, u32[]{:S(2)}) copy-start(bf16[32,4096]{1,0:T(8,128)(2,1)} %residual.1) | copy-start | bytes 786436
  18.2 1.9 %copy-start.3 = (f32[4096]{0:T(1024)S(1)}, f32[4096]{0:T(1024)}, u32[]{:S(2)}) copy-start(f32[4096]{0:T(1024)} %param.17) | copy-start | bytes 49156
  101.6 3.2 %copy-start.5 = (s32[32,8]{0,1:T(8,128)S(1)}, s32[32,8]{0,1:T(8,128)}, u32[]{:S(2)}) copy-start(s32[32,8]{0,1:T(8,128)} %param.20) | copy-start | bytes 3076
  102.2 4.0 %copy-start.4 = (f32[32,8]{0,1:T(8,128)S(1)}, f32[32,8]{0,1:T(8,128)}, u32[]{:S(2)}) copy-start(f32[32,8]{0,1:T(8,128)} %param.21) | copy-start | bytes 3076

commit v4 on v3

--- a/solution.py
+++ b/solution.py
@@ -47,6 +47,7 @@
     ret,
     tokens,
     normed,
+    flipped,
     units,
     hidden,
     sums,
@@ -214,8 +215,8 @@
 
         return action
 
-    tile = min(256, 2 * padded)
-    tiles = 2 * padded // tile
+    many = n_exp * tok_dev
+    slab = math.gcd(D, 512)
 
     def back_copy(place, index):
         slot = place * n_exp + index
@@ -230,31 +231,39 @@
     def back_local(slot):
         return pltpu.make_async_copy(hidden.at[slot], ret.at[slot], back_recv.at[slot])
 
-    def compute(place):
-        for index in range(n_exp):
-            row = tokens[place * n_exp + index].astype(jnp.float32)
-            square = jnp.mean(row * row, axis=1, keepdims=True)
-            normed[index] = (row * lax.rsqrt(square + 1e-06) * gain[...]).astype(jnp.bfloat16)
-        rows = normed[...]
-        if tok_dev % 16:
-            rows = rows.astype(jnp.float32).reshape(n_exp * tok_dev, D).astype(jnp.bfloat16)
-        else:
-            rows = rows.reshape(n_exp * tok_dev, D)
-        for which in range(2):
-            for index in range(tiles):
-                units[:, index * tile : (index + 1) * tile] = lax.dot_general(
-                    rows,
-                    weights[which, index * tile : (index + 1) * tile],
-                    (((1,), (1,)), ((), ())),
-                    preferred_element_type=jnp.float32,
+    def prepare(places):
+        for number, place in enumerate(places):
+            for index in range(n_exp):
+                row = tokens[place * n_exp + index].astype(jnp.float32)
+                square = jnp.mean(row * row, axis=1, keepdims=True)
+                row = row * lax.rsqrt(square + 1e-06) * gain[...]
+                if tok_dev % 16 == 0:
+                    row = row.astype(jnp.bfloat16)
+                normed[pl.ds(index * tok_dev, tok_dev)] = row.astype(normed.dtype)
+            for first in range(0, D, slab):
+                flipped[first : first + slab, number * many : (number + 1) * many] = (
+                    normed[:, first : first + slab].astype(jnp.bfloat16).T
                 )
-            gate, upper = units[:, :width], units[:, padded : padded + width]
-            result = gate / (1.0 + jnp.exp(-gate)) * upper
-            side = parity if which == 0 else 1 - parity
+
+    def expand(places, which):
+        amount = len(places) * many
+        for first in (0, padded):
+            units[first : first + padded, :amount] = jnp.dot(
+                weights[which, first : first + padded],
+                flipped[:, :amount],
+                preferred_element_type=jnp.float32,
+            )
+        gate, upper = units[:padded, :amount], units[padded:, :amount]
+        result = (gate / (1.0 + jnp.exp(-gate)) * upper).T
+        side = parity if which == 0 else 1 - parity
+        for number, place in enumerate(places):
             for index in range(n_exp):
+                first = number * many + index * tok_dev
                 hidden[place * n_exp + index, side] = result[
-                    index * tok_dev : (index + 1) * tok_dev
+                    first : first + tok_dev, :width
                 ].astype(jnp.bfloat16)
+
+    def give_back(place):
         for index in range(n_exp):
             slot = place * n_exp + index
 
@@ -265,6 +274,13 @@
             @pl.when(slot == mine)
             def _():
                 back_local(slot).start()
+
+    def compute(places):
+        prepare(places)
+        for which in range(2):
+            expand(places, which)
+        for place in places:
+            give_back(place)
 
     lag = 2
     for time in range(n_exp + half - 1 + lag * (CHUNKS - 1)):
@@ -278,19 +294,22 @@
                 for which in range(2):
                     own_copy(which).wait()
                     pair_copy(which).wait()
-                compute(pos)
+                prepare((pos,))
+                expand((pos,), 0)
+            if step == n_exp and piece == CHUNKS - 1:
+                expand((pos,), 1)
+                give_back(pos)
         for piece in range(CHUNKS):
             for hop in range(1, half):
                 step = time - lag * piece - hop
                 if 0 <= step < n_exp:
                     blocks_of(step, ring_step(hop, piece))
     for hop in range(1, half):
-        for way in (1, -1):
-            compute(ring_place((ring + way * hop + n_pos) % n_pos))
+        compute([ring_place((ring + way * hop + n_pos) % n_pos) for way in (1, -1)])
     for piece in range(CHUNKS):
         for step in range(n_exp):
             blocks_of(step, ring_step(half, piece))
-    compute(ring_place((ring + half) % n_pos))
+    compute((ring_place((ring + half) % n_pos),))
 
     for piece in range(CHUNKS):
         for step in range(1, n_exp):
@@ -331,7 +350,9 @@
     slots = n_pos * n_exp
     tok_dev = residual.shape[0]
     width = own_gate.shape[0]
-    padded = -(-width // 16) * 16
+    padded = -(-width // 128) * 128
+    many = n_exp * tok_dev
+    held = jnp.float32 if tok_dev % 16 else jnp.bfloat16
     half = n_pos // 2
     dma = pltpu.SemaphoreType.DMA
     vmem = pl.BlockSpec(memory_space=pltpu.VMEM)
@@ -345,8 +366,9 @@
         out_specs=(vmem, vmem),
         scratch_shapes=[
             pltpu.VMEM((slots, tok_dev, D), jnp.bfloat16),
-            pltpu.VMEM((n_exp, tok_dev, D), jnp.bfloat16),
-            pltpu.VMEM((n_exp * tok_dev, 2 * padded), jnp.float32),
+            pltpu.VMEM((many, D), held),
+            pltpu.VMEM((D, 2 * many), jnp.bfloat16),
+            pltpu.VMEM((2 * padded, 2 * many), jnp.float32),
             pltpu.VMEM((slots, 2, tok_dev, width), jnp.bfloat16),
             pltpu.VMEM((n_exp - 1, tok_dev, D), jnp.bfloat16),
             pltpu.VMEM((2, 2 * padded, D), jnp.bfloat16),

time: 108 us -> 107 us (level)
  Pallas kernels: 81.4 us -> 79.8 us
    pallas_call x1, Pallas kernels: 81.4 us -> 79.8 us  [expert_layer(): pl.pallas_call(functools.partial(expert_kernel, n_pos, n_exp), out_shape=...]
where the time goes in v4:
time: 107 us; the launch traced here: 106 us
  Pallas kernels  79.8 us (75%)
  blocking collectives  11.3 us (11%)
  local copies, waits for them, and re-layouts  7.81 us (7%)
  other arithmetic  3.58 us (3%)
  matrix products  2.99 us (3%)
    pallas_call x1, Pallas kernels, expert_layer(): pl.pallas_call(functools.partial(expert_kernel, n_pos, n_exp), out_shape=...  79.8 us
    all_gather x1, blocking collectives, shards(): lax.all_gather(jnp.concatenate((own_keys, own_values), axis=1), 'ctx', ax...  11.3 us
    unnamed x18, local copies, waits for them, and re-layouts  2.43 us

profile of v4, /device:TPU:0, one launch (start us, length us, event | category | flops | bytes accessed | tf_op | source)
XLA Modules:
  0.0 106.3 jit_solution(5017786457664011957)
XLA Ops:
  0.6 0.0 copy-start
  0.7 0.8 constant_dynamic-slice_fusion
  1.5 11.3 %all_gather.3 = bf16[1024,256]{1,0:T(8,128)(2,1)S(1)} all-gather(bf16[128,256]{1,0:T(8,128)(2,1)S(1)} %pad_maximum_fusion), channel_id=1, replica_groups=mesh['ctx'=8,'exp'=4] {'ctx'}, dimensions={0}, use_global_device_ids=true | all-gather | bytes 589824 | tf_op jit(solution)/shard_map/all_gather | solution.py:427
  12.8 0.7 select_reduce_fusion.1
  13.6 0.7 select_reduce_fusion
  14.3 0.2 broadcast_compare_fusion
  14.6 0.0 copy-done
  14.6 0.0 slice-start
  14.6 0.8 fusion
  15.4 0.0 slice-start.1
  15.4 0.9 fusion.3
  16.3 0.9 fusion.17
  17.2 0.0 slice-done
  17.2 1.0 slice-done.1
  18.2 0.0 copy-start.1
  18.2 0.0 copy-start.2
  18.2 0.0 copy-start.3
  18.2 1.3 %convolution_convert_fusion = bf16[128,4096]{1,0:T(8,128)(2,1)S(1)} fusion(bf16[128,1024]{0,1:T(8,128)(2,1)S(1)} %bitcast.78, bf16[1024,4096]{1,0:T(8,128)(2,1)S(1)} %bitcast.76), kind=kOutput, calls=%fused_computation.1 | convolution fusion | flops 1074266112 | bytes 9699328 | tf_op jit(solution)/shard_map/dot_general | solution.py:464
  19.5 0.6 copy-done.1
  20.1 0.0 copy-done.2
  20.1 0.0 copy-done.3
  20.1 79.8 %shard_map.122 = (bf16[32,4096]{1,0:T(8,128)(2,1)S(1)}, bf16[16,2,32,384]{3,2,1,0:T(8,128)(2,1)S(1)}) custom-call(bf16[4,32,4096]{2,1,0:T(8,128)(2,1)S(1)} %bitcast.72, bf16[32,4096]{1,0:T(8,128)(2,1)S(1)} %copy-done.2, f32[1,4096]{1,0:T(1,128)S(1)} %bitcast.74, bf16[384,4096]{1,0:T(8,128)(2,1)S(1)} %bitcast.73, bf16[384,4096]{1,0:T(8,128)(2,1)} %bitcast.80), custom_call_target="tpu_custom_call" | custom-call | flops 6442450944 | bytes 8388608 | tf_op jit(solution)/shard_map/pallas_call | solution.py:359
  99.9 0.0 copy-start.5
  100.0 0.6 reshape.194
  100.6 0.0 copy-start.4
  100.6 1.6 %copy.30 = bf16[32,4,4,4,2,96]{5,4,3,2,1,0:T(2,128)(2,1)S(1)} copy(bf16[32,4,4,4,2,96]{5,2,0,4,1,3:T(4,128)(2,1)S(1)} %bitcast.77) | data formatting | bytes 1572864 | tf_op jit(solution)/shard_map/transpose | solution.py:476
  102.2 0.9 reshape.195
  103.1 0.0 copy-done.5
  103.1 0.1 copy.31
  103.2 0.1 reshape.196
  103.3 1.2 %gather_fusion = bf16[256,768]{1,0:T(8,128)(2,1)S(1)} fusion(bf16[512,768]{1,0:T(8,128)(2,1)S(1)} %reshape.195, s32[1024]{0:T(1024)S(1)} %pad_clamp_fusion), kind=kCustom, calls=%fused_computation | custom fusion | bytes 787456 | tf_op jit(solution)/shard_map/jit(_take)/gather | solution.py:478
  104.5 0.1 copy.29
  104.6 0.0 copy-done.4
  104.6 0.1 copy.32
  104.7 0.9 multiply_convert_fusion
  105.6 0.7 copy.44
  (12 shorter events, 0.1 us)
Async XLA Ops:
  0.6 13.9 %copy-start = (bf16[128,1024]{1,0:T(8,128)(2,1)S(1)}, bf16[128,1024]{1,0:T(8,128)(2,1)}, u32[]{:S(2)}) copy-start(bf16[128,1024]{1,0:T(8,128)(2,1)} %param.12) | copy-start | bytes 786436
  14.6 2.6 %slice-start = ((s8[8388608]{0:T(1024)(128)(4,1)}), s8[4194304]{0:T(1024)(128)(4,1)S(1)}, s32[]{:S(2)}) async-start(s8[8388608]{0:T(1024)(128)(4,1)} %bitcast.75), calls=%async_computation | async-start | bytes 8388608
  15.4 2.9 %slice-start.1 = ((s8[8388608]{0:T(1024)(128)(4,1)}), s8[4194304]{0:T(1024)(128)(4,1)S(1)}, s32[]{:S(2)}) async-start(s8[8388608]{0:T(1024)(128)(4,1)} %bitcast.75), calls=%async_computation.1 | async-start | bytes 8388608
  18.2 1.9 %copy-start.1 = (bf16[4,4096,96]{1,2,0:T(8,128)(2,1)S(1)}, bf16[4,4096,96]{1,2,0:T(8,128)(2,1)}, u32[]{:S(2)}) copy-start(bf16[4,4096,96]{1,2,0:T(8,128)(2,1)} %param.18) | copy-start | bytes 9437188
  18.2 1.9 %copy-start.2 = (bf16[32,4096]{1,0:T(8,128)(2,1)S(1)}, bf16[32,4096]{1,0:T(8,128)(2,1)}, u32[]{:S(2)}) copy-start(bf16[32,4096]{1,0:T(8,128)(2,1)} %residual.1) | copy-start | bytes 786436
  18.2 1.9 %copy-start.3 = (f32[4096]{0:T(1024)S(1)}, f32[4096]{0:T(1024)}, u32[]{:S(2)}) copy-start(f32[4096]{0:T(1024)} %param.17) | copy-start | bytes 49156
  99.9 3.2 %copy-start.5 = (s32[32,8]{0,1:T(8,128)S(1)}, s32[32,8]{0,1:T(8,128)}, u32[]{:S(2)}) copy-start(s32[32,8]{0,1:T(8,128)} %param.20) | copy-start | bytes 3076
  100.6 4.0 %copy-start.4 = (f32[32,8]{0,1:T(8,128)S(1)}, f32[32,8]{0,1:T(8,128)}, u32[]{:S(2)}) copy-start(f32[32,8]{0,1:T(8,128)} %param.21) | copy-start | bytes 3076

commit v5 on v4

--- a/solution.py
+++ b/solution.py
@@ -26,7 +26,7 @@
     return base * CH + rows % CH
 
 
-CHUNKS = 2
+CHUNKS = 1
 MESH = pl.DeviceIdType.MESH
 
 

time: 107 us -> 105 us (0.981)
  Pallas kernels: 79.8 us -> 78.6 us
    pallas_call x1, Pallas kernels: 79.8 us -> 78.6 us  [expert_layer(): pl.pallas_call(functools.partial(expert_kernel, n_pos, n_exp), out_shape=...]
where the time goes in v5:
time: 105 us
  Pallas kernels  78.6 us (75%)
  blocking collectives  11.3 us (11%)
  local copies, waits for them, and re-layouts  7.81 us (7%)
  other arithmetic  3.58 us (3%)
  matrix products  2.99 us (3%)
    pallas_call x1, Pallas kernels, expert_layer(): pl.pallas_call(functools.partial(expert_kernel, n_pos, n_exp), out_shape=...  78.6 us
    all_gather x1, blocking collectives, shards(): lax.all_gather(jnp.concatenate((own_keys, own_values), axis=1), 'ctx', ax...  11.3 us
    unnamed x18, local copies, waits for them, and re-layouts  2.43 us

profile of v5, /device:TPU:0, one launch (start us, length us, event | category | flops | bytes accessed | tf_op | source)
XLA Modules:
  0.0 105.1 jit_solution(3052894155265613505)
XLA Ops:
  0.6 0.0 copy-start
  0.7 0.8 constant_dynamic-slice_fusion
  1.5 11.3 %all_gather.3 = bf16[1024,256]{1,0:T(8,128)(2,1)S(1)} all-gather(bf16[128,256]{1,0:T(8,128)(2,1)S(1)} %pad_maximum_fusion), channel_id=1, replica_groups=mesh['ctx'=8,'exp'=4] {'ctx'}, dimensions={0}, use_global_device_ids=true | all-gather | bytes 589824 | tf_op jit(solution)/shard_map/all_gather | solution.py:427
  12.8 0.7 select_reduce_fusion.1
  13.6 0.7 select_reduce_fusion
  14.3 0.2 broadcast_compare_fusion
  14.6 0.0 copy-done
  14.6 0.0 slice-start
  14.6 0.8 fusion
  15.4 0.0 slice-start.1
  15.4 0.9 fusion.3
  16.3 0.9 fusion.17
  17.2 0.0 slice-done
  17.2 1.0 slice-done.1
  18.2 0.0 copy-start.1
  18.2 0.0 copy-start.2
  18.2 0.0 copy-start.3
  18.2 1.3 %convolution_convert_fusion = bf16[128,4096]{1,0:T(8,128)(2,1)S(1)} fusion(bf16[128,1024]{0,1:T(8,128)(2,1)S(1)} %bitcast.78, bf16[1024,4096]{1,0:T(8,128)(2,1)S(1)} %bitcast.76), kind=kOutput, calls=%fused_computation.1 | convolution fusion | flops 1074266112 | bytes 9699328 | tf_op jit(solution)/shard_map/dot_general | solution.py:464
  19.5 0.6 copy-done.1
  20.1 0.0 copy-done.2
  20.1 0.0 copy-done.3
  20.1 78.6 %shard_map.122 = (bf16[32,4096]{1,0:T(8,128)(2,1)S(1)}, bf16[16,2,32,384]{3,2,1,0:T(8,128)(2,1)S(1)}) custom-call(bf16[4,32,4096]{2,1,0:T(8,128)(2,1)S(1)} %bitcast.72, bf16[32,4096]{1,0:T(8,128)(2,1)S(1)} %copy-done.2, f32[1,4096]{1,0:T(1,128)S(1)} %bitcast.74, bf16[384,4096]{1,0:T(8,128)(2,1)S(1)} %bitcast.73, bf16[384,4096]{1,0:T(8,128)(2,1)} %bitcast.80), custom_call_target="tpu_custom_call" | custom-call | flops 6442450944 | bytes 8388608 | tf_op jit(solution)/shard_map/pallas_call | solution.py:359
  98.7 0.0 copy-start.5
  98.7 0.6 reshape.194
  99.3 0.0 copy-start.4
  99.3 1.6 %copy.30 = bf16[32,4,4,4,2,96]{5,4,3,2,1,0:T(2,128)(2,1)S(1)} copy(bf16[32,4,4,4,2,96]{5,2,0,4,1,3:T(4,128)(2,1)S(1)} %bitcast.77) | data formatting | bytes 1572864 | tf_op jit(solution)/shard_map/transpose | solution.py:476
  101.0 0.9 reshape.195
  101.9 0.0 copy-done.5
  101.9 0.1 copy.31
  102.0 0.1 reshape.196
  102.1 1.2 %gather_fusion = bf16[256,768]{1,0:T(8,128)(2,1)S(1)} fusion(bf16[512,768]{1,0:T(8,128)(2,1)S(1)} %reshape.195, s32[1024]{0:T(1024)S(1)} %pad_clamp_fusion), kind=kCustom, calls=%fused_computation | custom fusion | bytes 787456 | tf_op jit(solution)/shard_map/jit(_take)/gather | solution.py:478
  103.3 0.1 copy.29
  103.4 0.0 copy-done.4
  103.4 0.1 copy.32
  103.4 0.9 multiply_convert_fusion
  104.4 0.7 copy.44
  (12 shorter events, 0.1 us)
Async XLA Ops:
  0.6 13.9 %copy-start = (bf16[128,1024]{1,0:T(8,128)(2,1)S(1)}, bf16[128,1024]{1,0:T(8,128)(2,1)}, u32[]{:S(2)}) copy-start(bf16[128,1024]{1,0:T(8,128)(2,1)} %param.12) | copy-start | bytes 786436
  14.6 2.6 %slice-start = ((s8[8388608]{0:T(1024)(128)(4,1)}), s8[4194304]{0:T(1024)(128)(4,1)S(1)}, s32[]{:S(2)}) async-start(s8[8388608]{0:T(1024)(128)(4,1)} %bitcast.75), calls=%async_computation | async-start | bytes 8388608
  15.4 2.9 %slice-start.1 = ((s8[8388608]{0:T(1024)(128)(4,1)}), s8[4194304]{0:T(1024)(128)(4,1)S(1)}, s32[]{:S(2)}) async-start(s8[8388608]{0:T(1024)(128)(4,1)} %bitcast.75), calls=%async_computation.1 | async-start | bytes 8388608
  18.2 1.9 %copy-start.1 = (bf16[4,4096,96]{1,2,0:T(8,128)(2,1)S(1)}, bf16[4,4096,96]{1,2,0:T(8,128)(2,1)}, u32[]{:S(2)}) copy-start(bf16[4,4096,96]{1,2,0:T(8,128)(2,1)} %param.18) | copy-start | bytes 9437188
  18.2 1.9 %copy-start.2 = (bf16[32,4096]{1,0:T(8,128)(2,1)S(1)}, bf16[32,4096]{1,0:T(8,128)(2,1)}, u32[]{:S(2)}) copy-start(bf16[32,4096]{1,0:T(8,128)(2,1)} %residual.1) | copy-start | bytes 786436
  18.2 1.9 %copy-start.3 = (f32[4096]{0:T(1024)S(1)}, f32[4096]{0:T(1024)}, u32[]{:S(2)}) copy-start(f32[4096]{0:T(1024)} %param.17) | copy-start | bytes 49156
  98.7 3.2 %copy-start.5 = (s32[32,8]{0,1:T(8,128)S(1)}, s32[32,8]{0,1:T(8,128)}, u32[]{:S(2)}) copy-start(s32[32,8]{0,1:T(8,128)} %param.20) | copy-start | bytes 3076
  99.3 4.0 %copy-start.4 = (f32[32,8]{0,1:T(8,128)S(1)}, f32[32,8]{0,1:T(8,128)}, u32[]{:S(2)}) copy-start(f32[32,8]{0,1:T(8,128)} %param.21) | copy-start | bytes 3076
